TPU v7x, 256 devices: a whole 4x4x8 slice. The times are simulated.
256 devices in a mesh: tm: 8 (over z_lo, x), height: 32 (over z_hi, y, core).
Axes of the slice: x: 4, y: 4, z: 8 (z_hi: 4, z_lo: 2; z = z_hi * 2 + z_lo), core: 2. Of those that a mesh axis runs over, the one named last changes fastest.
Arguments:
- inputs: bfloat16 [16, 768, 4, 1024], P('tm', 'height'), may hold values from -24 to 24
- w_query: bfloat16 [1024, 1024], replicated, may hold values from -0.1875 to 0.1875
- w_key: bfloat16 [1024, 1024], replicated, may hold values from -0.1875 to 0.1875
- w_value: bfloat16 [1024, 1024], replicated, may hold values from -0.1875 to 0.1875
- w_out: bfloat16 [1024, 1024], replicated, may hold values from -0.1875 to 0.1875
- grad_out: bfloat16 [16, 768, 4, 1024], P('tm', 'height'), may hold values from -6 to 6
Outputs:
- attended: bfloat16 [16, 768, 4, 1024], P('tm', 'height')
- grad_in: bfloat16 [16, 768, 4, 1024], P('tm', 'height')
All inputs are finite; a program needn't handle non-finite values.
Results may differ from a plain program's by a relative error of at most 0.03.
The roundings to bfloat16 on the way count: a program that leaves them out, or rounds other values in their place, can miss the bound.
Values may be sent and summed in bfloat16 or wider, within the bound.
No kernel may reach another device: no remote copies, remote signals or barrier semaphores. Data moves between devices by JAX's collectives and lax.ppermute only.
A program may use at most 128 MiB of HBM per device.

v0:
```python
import functools

import jax
import jax.numpy as jnp
from jax import lax
from jax.experimental import pallas as pl
from jax.experimental.pallas import tpu as pltpu
from jax.sharding import PartitionSpec as P

HD = 64
RT = 2
RH = 7
BR = 8
WC = 4
GW = 256
VMEM_LIMIT = 56 * 1024 * 1024
NEG = -1e30
F32 = jnp.float32
BF16 = jnp.bfloat16


def nn(a, b):
    return lax.dot_general(a, b, (((1,), (0,)), ((), ())), preferred_element_type=F32)


def nt(a, b):
    return lax.dot_general(a, b, (((1,), (1,)), ((), ())), preferred_element_type=F32)


def tn(a, b):
    return lax.dot_general(a, b, (((0,), (0,)), ((), ())), preferred_element_type=F32)


def call(body, out_shapes, *args, scalars=False, scratch=()):
    specs = [pl.BlockSpec(memory_space=pltpu.VMEM) for _ in args]
    if scalars:
        specs[0] = pl.BlockSpec(memory_space=pltpu.SMEM)
    return pl.pallas_call(
        body,
        out_shape=[jax.ShapeDtypeStruct(s, d) for s, d in out_shapes],
        in_specs=specs,
        out_specs=[pl.BlockSpec(memory_space=pltpu.VMEM) for _ in out_shapes],
        scratch_shapes=list(scratch),
        compiler_params=pltpu.CompilerParams(vmem_limit_bytes=VMEM_LIMIT),
    )(*args)


def project(x, w_ref, out_ref, scale=None):
    groups, frames, rows, width = out_ref.shape
    for g in range(groups):
        y = nn(x, w_ref[:, g * width : (g + 1) * width])
        if scale is not None:
            y = y * scale
        out_ref[g] = y.astype(BF16).reshape(frames, rows, width)


def project_t(x, w_ref, out_ref):
    groups, frames, rows, width = out_ref.shape
    for g in range(groups):
        y = nt(x, w_ref[g * width : (g + 1) * width, :])
        out_ref[g] = y.astype(BF16).reshape(frames, rows, width)


def flat(ref):
    return ref[...].reshape(-1, ref.shape[-1])


def own_kernel(x_ref, gr_ref, wq_ref, wk_ref, wv_ref, wo_ref, q_ref, k_ref, v_ref, ga_ref):
    x = flat(x_ref)
    project(x, wk_ref, k_ref)
    project(x, wv_ref, v_ref)
    project(x, wq_ref, q_ref, HD**-0.5)
    project_t(flat(gr_ref), wo_ref, ga_ref)


def side_kernel(xa_ref, xb_ref, wq_ref, wk_ref, wv_ref, q_ref, k_ref, v_ref):
    x = jnp.concatenate([flat(xa_ref), flat(xb_ref)], axis=0)
    project(x, wk_ref, k_ref)
    project(x, wv_ref, v_ref)
    project(x, wq_ref, q_ref, HD**-0.5)


def side_grad_kernel(ga_ref, gb_ref, wo_ref, out_ref):
    g = jnp.concatenate([flat(ga_ref), flat(gb_ref)], axis=0)
    project_t(g, wo_ref, out_ref)


def spread(block):
    heads = block.shape[1] // HD
    lane = lax.broadcasted_iota(jnp.int32, block.shape, 1) // HD
    zero = jnp.zeros_like(block)
    return jnp.concatenate([jnp.where(lane == h, block, zero) for h in range(heads)], axis=0)


def window(rb, own, top, bottom):
    half = BR * WC
    if rb == 0:
        return jnp.concatenate([top, own[:, : 2 * half]], axis=1)
    if rb == 1:
        return own
    return jnp.concatenate([own[:, half:], bottom], axis=1)


def row_bias(rb, h, n_rows, rows):
    span = 3 * BR * WC
    w = lax.broadcasted_iota(jnp.int32, (span, GW), 0) // WC
    r = (lax.broadcasted_iota(jnp.int32, (span, GW), 1) % (BR * WC)) // WC
    diff = w - r - BR
    glob = h * rows + rb * BR + w - BR
    ok = (diff >= -RH) & (diff <= RH) & (glob >= 0) & (glob < n_rows)
    return jnp.where(ok, F32(0), F32(NEG))


def frame_bias(key_off, query_off, tm, n_frames, frames):
    fq = (lax.broadcasted_iota(jnp.int32, (1, GW), 1) // (BR * WC)) % 2 + query_off
    diff = key_off - fq
    glob = tm * frames + key_off
    ok = (diff >= -RT) & (diff <= RT) & (glob >= 0) & (glob < n_frames)
    return jnp.where(ok, F32(0), F32(NEG))


def slot_offsets(tm):
    odd = tm % 2
    return 4 * odd - 2, 2 - 4 * odd


def forward_kernel(
    n_frames, n_rows, frames, rows,
    info_ref, xe_ref, xo_ref, wk_ref, wv_ref, q_ref, ga_ref, k_ref, v_ref, ks_ref, vs_ref,
    stats_ref, mixed_ref, dq_ref, dk_ref, dv_ref, krow_ref, vrow_ref,
    bias_ref, kh_ref, vh_ref,
):
    tm, h = info_ref[0], info_ref[1]
    half = BR * WC
    groups = q_ref.shape[0]
    h_odd = h % 2
    for x_ref, side in ((xe_ref, 1 - h_odd), (xo_ref, h_odd)):
        x = flat(x_ref)
        for g in range(groups):
            kh_ref[side, g] = nn(x, wk_ref[:, g * GW : (g + 1) * GW]).astype(BF16).reshape(6, half, GW)
            vh_ref[side, g] = nn(x, wv_ref[:, g * GW : (g + 1) * GW]).astype(BF16).reshape(6, half, GW)
    for side in range(2):
        for g in range(groups):
            krow_ref[side, g] = kh_ref[side, g, 2:4]
            vrow_ref[side, g] = vh_ref[side, g, 2:4]
    off_a, off_b = slot_offsets(tm)
    offsets = (off_a, off_a + 1, 0, 1, off_b, off_b + 1)
    for rb in range(3):
        base = row_bias(rb, h, n_rows, rows)
        for s in range(6):
            bias_ref[rb, s] = base + frame_bias(offsets[s], 0, tm, n_frames, frames)
    dk_ref[...] = jnp.zeros_like(dk_ref)
    dv_ref[...] = jnp.zeros_like(dv_ref)
    pick = (
        lax.broadcasted_iota(jnp.int32, (64, GW), 0) == lax.broadcasted_iota(jnp.int32, (64, GW), 1) % 64
    ).astype(F32).astype(BF16)
    diag = (
        lax.broadcasted_iota(jnp.int32, (GW, GW), 0) // HD == lax.broadcasted_iota(jnp.int32, (GW, GW), 1) // 64
    )

    def group(g, carry):
        kall = jnp.concatenate([ks_ref[g, 0:2], k_ref[g], ks_ref[g, 2:4]], axis=0)
        vall = jnp.concatenate([vs_ref[g, 0:2], v_ref[g], vs_ref[g, 2:4]], axis=0)
        for rb in range(3):
            at = slice(rb * half, (rb + 1) * half)
            kw = window(rb, kall, kh_ref[0, g], kh_ref[1, g]).reshape(-1, GW)
            vw = window(rb, vall, vh_ref[0, g], vh_ref[1, g]).reshape(-1, GW)
            qs = spread(q_ref[g, :, at, :].reshape(64, GW))
            gs = spread(ga_ref[g, :, at, :].reshape(64, GW))
            s = nt(kw, qs) + bias_ref[rb].reshape(-1, GW)
            m = jnp.max(s, axis=0, keepdims=True)
            e = jnp.exp(s - m)
            rl = 1.0 / jnp.sum(e, axis=0, keepdims=True)
            dp = nt(vw, gs)
            delta = jnp.sum(e * dp, axis=0, keepdims=True) * rl
            p = e * rl
            pb = p.astype(BF16)
            ds = (p * (dp - delta)).astype(BF16)
            u = g * 3 + rb
            stats_ref[u, 0:1, :] = m
            stats_ref[u, 1:2, :] = rl
            stats_ref[u, 2:3, :] = delta
            stats_ref[u, 3:4, :] = delta
            mt = jnp.where(diag, tn(vw, pb), 0.0).astype(BF16)
            mixed_ref[g, :, at, :] = nt(pick, mt).astype(BF16).reshape(2, half, GW)
            qt = jnp.where(diag, tn(kw, ds) * (HD**-0.5), 0.0).astype(BF16)
            dq_ref[g, :, at, :] = nt(pick, qt).astype(BF16).reshape(2, half, GW)
            mid = slice(2 * 3 * half, 4 * 3 * half)
            to = slice(rb * half, (rb + 3) * half)
            dk_ref[g, :, to, :] += nn(ds[mid], qs).reshape(2, 3 * half, GW)
            dv_ref[g, :, to, :] += nn(pb[mid], gs).reshape(2, 3 * half, GW)
        return carry

    lax.fori_loop(0, groups, group, 0)


def middle_kernel(mixed_ref, dq_ref, wo_ref, wq_ref, att_ref, dxq_ref):
    groups = mixed_ref.shape[0]
    mixed = jnp.concatenate([mixed_ref[g].reshape(-1, GW) for g in range(groups)], axis=1)
    att_ref[...] = nn(mixed, wo_ref[...]).astype(BF16).reshape(att_ref.shape)
    dq = jnp.concatenate([dq_ref[g].reshape(-1, GW) for g in range(groups)], axis=1)
    dxq_ref[...] = nt(dq, wq_ref[...]).reshape(dxq_ref.shape)


def backward_kernel(
    n_frames, n_rows, frames, rows,
    info_ref, sa_ref, sb_ref, qs_ref, gs_ref, k_ref, v_ref, krow_ref, vrow_ref, dk_ref, dv_ref, dxq_ref,
    wk_ref, wv_ref,
    own_ref, me_ref, mo_ref,
    bias_ref, dka_ref, dva_ref, edge_ref,
):
    tm, h = info_ref[0], info_ref[1]
    half = BR * WC
    groups = k_ref.shape[0]
    off_a, off_b = slot_offsets(tm)
    for rb in range(3):
        base = row_bias(rb, h, n_rows, rows)
        for p, off in enumerate((off_a, off_b)):
            for f in range(2):
                bias_ref[p, rb, f] = base + frame_bias(f, off, tm, n_frames, frames)
    dka_ref[...] = dk_ref[...]
    dva_ref[...] = dv_ref[...]

    def group(g, carry):
        for rb in range(3):
            at = slice(rb * half, (rb + 1) * half)
            to = slice(rb * half, (rb + 3) * half)
            kw = window(rb, k_ref[g], krow_ref[0, g], krow_ref[1, g]).reshape(-1, GW)
            vw = window(rb, v_ref[g], vrow_ref[0, g], vrow_ref[1, g]).reshape(-1, GW)
            u = g * 3 + rb
            for p, s_ref in enumerate((sa_ref, sb_ref)):
                qs = spread(qs_ref[g, 2 * p : 2 * p + 2, at, :].reshape(64, GW))
                gs = spread(gs_ref[g, 2 * p : 2 * p + 2, at, :].reshape(64, GW))
                m, rl, delta = s_ref[u, 0:1, :], s_ref[u, 1:2, :], s_ref[u, 2:3, :]
                s = nt(kw, qs) + bias_ref[p, rb].reshape(-1, GW)
                pr = jnp.exp(s - m) * rl
                ds = (pr * (nt(vw, gs) - delta)).astype(BF16)
                dka_ref[g, :, to, :] += nn(ds, qs).reshape(2, 3 * half, GW)
                dva_ref[g, :, to, :] += nn(pr.astype(BF16), gs).reshape(2, 3 * half, GW)
        return carry

    lax.fori_loop(0, groups, group, 0)
    dk = jnp.concatenate([dka_ref[g].astype(BF16).reshape(-1, GW) for g in range(groups)], axis=1)
    dv = jnp.concatenate([dva_ref[g].astype(BF16).reshape(-1, GW) for g in range(groups)], axis=1)
    dx = (nt(dk, wk_ref[...]) + nt(dv, wv_ref[...])).reshape(2, 5 * half, -1)
    own_ref[...] = dx[:, half : 4 * half] + dxq_ref[...]
    edge_ref[0] = dx[:, :half].astype(BF16)
    edge_ref[1] = dx[:, 4 * half :].astype(BF16)
    h_odd = h % 2
    me_ref[...] = edge_ref[1 - h_odd]
    mo_ref[...] = edge_ref[h_odd]


def last_kernel(info_ref, own_ref, re_ref, ro_ref, out_ref, acc_ref):
    half = BR * WC
    h_odd = info_ref[1] % 2
    acc_ref[...] = own_ref[...]
    for r_ref, side in ((re_ref, 1 - h_odd), (ro_ref, h_odd)):
        at = pl.ds(pl.multiple_of(side * (2 * half), half), half)
        acc_ref[:, at, :] += r_ref[...].astype(F32)
    out_ref[...] = acc_ref[...].astype(BF16)


def swap_pairs(count, first):
    pairs = [(i, i + 1) for i in range(first, count - 1, 2)]
    return pairs + [(b, a) for a, b in pairs]


def swap(block, axis, first):
    return lax.ppermute(block, axis, swap_pairs(lax.axis_size(axis), first))


def shards(inputs, w_query, w_key, w_value, w_out, grad_out):
    frames, rows, cols, width = inputs.shape
    groups = width // GW
    tokens = rows * cols
    half = BR * WC
    tm, h = lax.axis_index("tm"), lax.axis_index("height")
    n_frames, n_rows = lax.axis_size("tm") * frames, lax.axis_size("height") * rows
    info = jnp.stack([tm, h]).astype(jnp.int32)
    dims = (n_frames, n_rows, frames, rows)

    x = inputs.reshape(frames, tokens, width)
    grad = grad_out.reshape(frames, tokens, width)
    xa = swap(x, "tm", 1)
    xb = swap(x, "tm", 0)
    ga = swap(grad, "tm", 1)
    gb = swap(grad, "tm", 0)

    def edge(block, bottom):
        return lax.dynamic_slice_in_dim(block, bottom * (tokens - half), half, axis=1)

    h_odd = h % 2
    wide = jnp.concatenate([xa, x, xb], axis=0)
    xo = swap(edge(wide, h_odd), "height", 1)
    xe = swap(edge(wide, 1 - h_odd), "height", 0)

    group_shape = ((groups, frames, tokens, GW), BF16)
    side_shape = ((groups, 2 * frames, tokens, GW), BF16)
    q, k, v, ga_own = call(own_kernel, [group_shape] * 4, x, grad, w_query, w_key, w_value, w_out)
    q_side, k_side, v_side = call(side_kernel, [side_shape] * 3, xa, xb, w_query, w_key, w_value)
    (ga_side,) = call(side_grad_kernel, [side_shape], ga, gb, w_out)

    acc_shape = (groups, frames, tokens + 2 * half, GW)
    row_shape = ((2, groups, frames, half, GW), BF16)
    stats, mixed, dq, dk, dv, k_row, v_row = call(
        functools.partial(forward_kernel, *dims),
        [((3 * groups, 4, GW), F32), group_shape, group_shape, (acc_shape, F32), (acc_shape, F32), row_shape, row_shape],
        info, xe, xo, w_key, w_value, q, ga_own, k, v, k_side, v_side,
        scalars=True,
        scratch=[
            pltpu.VMEM((3, 6, tokens, GW), F32),
            pltpu.VMEM((2, groups, 6, half, GW), BF16),
            pltpu.VMEM((2, groups, 6, half, GW), BF16),
        ],
    )
    sa = swap(stats, "tm", 1)
    sb = swap(stats, "tm", 0)
    token_shape = (frames, tokens, width)
    attended, dxq = call(
        middle_kernel, [(token_shape, BF16), (token_shape, F32)], mixed, dq, w_out, w_query
    )
    own, me, mo = call(
        functools.partial(backward_kernel, *dims),
        [(token_shape, F32), ((frames, half, width), BF16), ((frames, half, width), BF16)],
        info, sa, sb, q_side, ga_side, k, v, k_row, v_row, dk, dv, dxq, w_key, w_value,
        scalars=True,
        scratch=[
            pltpu.VMEM((2, 3, 2, tokens, GW), F32),
            pltpu.VMEM(acc_shape, F32),
            pltpu.VMEM(acc_shape, F32),
            pltpu.VMEM((2, frames, half, width), BF16),
        ],
    )
    ro = swap(mo, "height", 1)
    re = swap(me, "height", 0)
    (grad_in,) = call(
        last_kernel, [(token_shape, BF16)], info, own, re, ro, scalars=True, scratch=[pltpu.VMEM(token_shape, F32)]
    )
    return (attended.reshape(inputs.shape), grad_in.reshape(inputs.shape))


def solution(mesh):
    placed = (P("tm", "height", None, None), P(), P(), P(), P(), P("tm", "height", None, None))
    return jax.shard_map(
        shards,
        mesh=mesh,
        in_specs=placed,
        out_specs=(P("tm", "height", None, None), P("tm", "height", None, None)),
        check_vma=False,
    )
```

profile of v0, /device:TPU:89, one launch (start us, length us, event | category | flops | bytes accessed | tf_op | source)
XLA Modules:
  0.0 111.8 jit_solution(6386934857717844713)
XLA Ops:
  0.6 1.1 reshape.16.x_ref
  1.7 0.7 collective-permute-start
  2.4 3.7 %collective-permute-start.1 = (bf16[2,96,1024]{2,1,0:T(8,128)(2,1)S(1)}, bf16[2,96,1024]{2,1,0:T(8,128)(2,1)S(1)}, u32[]{:S(2)}, u32[]{:S(2)}) collective-permute-start(bf16[2,96,1024]{2,1,0:T(8,128)(2,1)S(1)} %reshape.16.x_ref), channel_id=1, source_target_pairs={{0,32},{64,96},{128,160},{192,224},{32,0},{96,64},{160,128},{224,1... | collective-permute-start | bytes 1179656 | tf_op jit(solution)/shard_map/ppermute | solution.py:270
  6.2 8.4 %collective-permute-done.1.xb_ref = bf16[2,96,1024]{2,1,0:T(8,128)(2,1)S(1)} collective-permute-done((bf16[2,96,1024]{2,1,0:T(8,128)(2,1)S(1)}, bf16[2,96,1024]{2,1,0:T(8,128)(2,1)S(1)}, u32[]{:S(2)}, u32[]{:S(2)}) %collective-permute-start.1) | collective-permute-done | bytes 393248 | tf_op jit(solution)/shard_map/ppermute | solution.py:270
  14.7 0.1 constant_dynamic-slice_fusion
  14.8 0.6 copy-done.3
  15.4 1.5 %collective-permute-start.2 = (bf16[6,32,1024]{2,1,0:T(8,128)(2,1)S(1)}, bf16[6,32,1024]{2,1,0:T(8,128)(2,1)S(1)}, u32[]{:S(2)}, u32[]{:S(2)}) collective-permute-start(bf16[6,32,1024]{2,1,0:T(8,128)(2,1)S(1)} %get-tuple-element.41), channel_id=1, source_target_pairs={{0,1},{2,3},{4,5},{6,7},{8,9},{10,11},{12,13},{14,15},{16,17},{18,... | collective-permute-start | bytes 1179656 | tf_op jit(solution)/shard_map/ppermute | solution.py:270
  17.0 5.6 %collective-permute-start.3 = (bf16[6,32,1024]{2,1,0:T(8,128)(2,1)S(1)}, bf16[6,32,1024]{2,1,0:T(8,128)(2,1)S(1)}, u32[]{:S(2)}, u32[]{:S(2)}) collective-permute-start(bf16[6,32,1024]{2,1,0:T(8,128)(2,1)S(1)} %get-tuple-element.40), channel_id=1, source_target_pairs={{1,2},{3,4},{5,6},{7,8},{9,10},{11,12},{13,14},{15,16},{17,18},{19... | collective-permute-start | bytes 1179656 | tf_op jit(solution)/shard_map/ppermute | solution.py:270
  22.6 0.1 reshape.17.gr_ref
  22.8 0.7 collective-permute-start.6
  23.4 3.0 %collective-permute-start.7 = (bf16[2,96,1024]{2,1,0:T(8,128)(2,1)S(1)}, bf16[2,96,1024]{2,1,0:T(8,128)(2,1)S(1)}, u32[]{:S(2)}, u32[]{:S(2)}) collective-permute-start(bf16[2,96,1024]{2,1,0:T(8,128)(2,1)S(1)} %reshape.17.gr_ref), channel_id=1, source_target_pairs={{0,32},{64,96},{128,160},{192,224},{32,0},{96,64},{160,128},{224,1... | collective-permute-start | bytes 1179656 | tf_op jit(solution)/shard_map/ppermute | solution.py:270
  26.5 6.5 %shard_map.77 = (bf16[4,2,96,256]{3,2,1,0:T(8,128)(2,1)}, bf16[4,2,96,256]{3,2,1,0:T(8,128)(2,1)}, bf16[4,2,96,256]{3,2,1,0:T(8,128)(2,1)}, bf16[4,2,96,256]{3,2,1,0:T(8,128)(2,1)}) custom-call(bf16[2,96,1024]{2,1,0:T(8,128)(2,1)} %copy-done, bf16[2,96,1024]{2,1,0:T(8,128)(2,1)} %copy-done.1, bf16[1024,1024]{1,0:T(8,128)(2,1)} %wq_ref.5, ...), custom_call_target="tpu_custom_call" | custom-call | tf_op jit(solution)/shard_map/pallas_call | solution.py:38
  33.0 0.6 pad_add_fusion.info_ref
  33.6 6.6 %shard_map.78 = (bf16[4,4,96,256]{3,2,1,0:T(8,128)(2,1)}, bf16[4,4,96,256]{3,2,1,0:T(8,128)(2,1)}, bf16[4,4,96,256]{3,2,1,0:T(8,128)(2,1)}) custom-call(bf16[2,96,1024]{2,1,0:T(8,128)(2,1)} %copy-done.2, bf16[2,96,1024]{2,1,0:T(8,128)(2,1)} %copy-done.3, bf16[1024,1024]{1,0:T(8,128)(2,1)} %wq_ref.5, bf16[1024,1024]{1,0:T(8,128)(2,1)} %wk_ref.7, ...), custom_call_target="tpu_custom_call" | custom-call | tf_op jit(solution)/shard_map/pallas_call | solution.py:38
  40.2 0.7 copy-done.4
  41.0 0.1 copy-done.5
  41.1 23.9 %shard_map.79 = (f32[12,4,256]{2,1,0:T(4,128)}, bf16[4,2,96,256]{3,2,1,0:T(8,128)(2,1)}, bf16[4,2,96,256]{3,2,1,0:T(8,128)(2,1)}, f32[4,2,160,256]{3,2,1,0:T(8,1...) custom-call(s32[2]{0:T(128)} %pad_add_fusion.info_ref, ...), custom_call_target="tpu_custom_call" | custom-call | tf_op jit(solution)/shard_map/pallas_call | solution.py:38
  65.0 0.7 collective-permute-start.4
  65.6 5.8 %collective-permute-start.5 = (f32[12,4,256]{2,1,0:T(4,128)}, f32[12,4,256]{2,1,0:T(4,128)S(1)}, u32[]{:S(2)}, u32[]{:S(2)}) collective-permute-start(f32[12,4,256]{2,1,0:T(4,128)} %get-tuple-element.30), channel_id=1, source_target_pairs={{0,32},{64,96},{128,160},{192,224},{32,0},{96,64},{160,128},{224,1... | collective-permute-start | bytes 147464 | tf_op jit(solution)/shard_map/ppermute | solution.py:270
  71.4 0.7 copy-done.6
  72.1 0.7 copy-done.7
  72.9 3.7 %shard_map.81.gs_ref = bf16[4,4,96,256]{3,2,1,0:T(8,128)(2,1)} custom-call(bf16[2,96,1024]{2,1,0:T(8,128)(2,1)} %copy-done.6, bf16[2,96,1024]{2,1,0:T(8,128)(2,1)} %copy-done.7, bf16[1024,1024]{1,0:T(8,128)(2,1)} %wo_ref.5), custom_call_target="tpu_custom_call" | custom-call | tf_op jit(solution)/shard_map/pallas_call | solution.py:38
  76.6 4.6 %shard_map.80 = (bf16[2,96,1024]{2,1,0:T(8,128)(2,1)}, f32[2,96,1024]{2,1,0:T(8,128)}) custom-call(bf16[4,2,96,256]{3,2,1,0:T(8,128)(2,1)} %get-tuple-element.27.mixed_ref, bf16[4,2,96,256]{3,2,1,0:T(8,128)(2,1)} %get-tuple-element.28.dq_ref, bf16[1024,1024]{1,0:T(8,128)(2,1)} %wo_ref.5, bf16[1024,1024]{1,0:T(8,128)(2,1)} %wq_ref.5), custom_call_target="tpu_custom_call" | custom-call | tf_op jit(solution)/shard_map/pallas_call | solution.py:38
  81.3 0.6 copy-done.12
  81.9 0.0 copy-done.13
  81.9 13.2 %shard_map.82 = (f32[2,96,1024]{2,1,0:T(8,128)}, bf16[2,32,1024]{2,1,0:T(8,128)(2,1)}, bf16[2,32,1024]{2,1,0:T(8,128)(2,1)}) custom-call(s32[2]{0:T(128)} %pad_add_fusion.info_ref, f32[12,4,256]{2,1,0:T(4,128)} %copy-done.12, f32[12,4,256]{2,1,0:T(4,128)} %copy-done.13, bf16[4,4,96,256]{3,2,1,0:T(8,128)(2,1)} %get-tuple-element.31.qs_ref, ...), custom_call_target="tpu_custom_call" | custom-call | tf_op jit(solution)/shard_map/pallas_call | solution.py:38
  95.1 5.3 %collective-permute-start.9 = (bf16[2,32,1024]{2,1,0:T(8,128)(2,1)}, bf16[2,32,1024]{2,1,0:T(8,128)(2,1)S(1)}, u32[]{:S(2)}, u32[]{:S(2)}) collective-permute-start(bf16[2,32,1024]{2,1,0:T(8,128)(2,1)} %get-tuple-element.39), channel_id=1, source_target_pairs={{1,2},{3,4},{5,6},{7,8},{9,10},{11,12},{13,14},{15,16},{17,18},{19... | collective-permute-start | bytes 393224 | tf_op jit(solution)/shard_map/ppermute | solution.py:270
  100.4 0.9 reshape.18
  101.3 5.8 %collective-permute-done.9.ro_ref = bf16[2,32,1024]{2,1,0:T(8,128)(2,1)S(1)} collective-permute-done((bf16[2,32,1024]{2,1,0:T(8,128)(2,1)}, bf16[2,32,1024]{2,1,0:T(8,128)(2,1)S(1)}, u32[]{:S(2)}, u32[]{:S(2)}) %collective-permute-start.9) | collective-permute-done | bytes 131104 | tf_op jit(solution)/shard_map/ppermute | solution.py:270
  107.2 0.6 copy-done.11
  107.8 2.1 %shard_map.83 = bf16[2,96,1024]{2,1,0:T(8,128)(2,1)} custom-call(s32[2]{0:T(128)} %pad_add_fusion.info_ref, f32[2,96,1024]{2,1,0:T(8,128)} %get-tuple-element.37.own_ref, bf16[2,32,1024]{2,1,0:T(8,128)(2,1)} %copy-done.10, bf16[2,32,1024]{2,1,0:T(8,128)(2,1)} %copy-done.11), custom_call_target="tpu_custom_call" | custom-call | tf_op jit(solution)/shard_map/pallas_call | solution.py:38
  110.0 1.9 %reshape.19 = bf16[2,24,4,1024]{3,2,1,0:T(4,128)(2,1)} reshape(bf16[2,96,1024]{2,1,0:T(8,128)(2,1)} %shard_map.83) | data formatting | bytes 786432 | tf_op jit(solution)/shard_map/reshape | solution.py:340
  (32 shorter events, 0.1 us)
Async XLA Ops:
  1.7 13.0 %copy-start = (bf16[2,96,1024]{2,1,0:T(8,128)(2,1)}, bf16[2,96,1024]{2,1,0:T(8,128)(2,1)S(1)}, u32[]{:S(2)}) copy-start(bf16[2,96,1024]{2,1,0:T(8,128)(2,1)S(1)} %reshape.16.x_ref) | copy-start | bytes 1179652
  1.7 4.4 %collective-permute-start = (bf16[2,96,1024]{2,1,0:T(8,128)(2,1)S(1)}, bf16[2,96,1024]{2,1,0:T(8,128)(2,1)S(1)}, u32[]{:S(2)}, u32[]{:S(2)}) collective-permute-start(bf16[2,96,1024]{2,1,0:T(8,128)(2,1)S(1)} %reshape.16.x_ref), channel_id=1, source_target_pairs={{32,64},{96,128},{160,192},{64,32},{128,96},{192,160},{33,65},{97,... | collective-permute-start | bytes 1179656 | tf_op jit(solution)/shard_map/ppermute | solution.py:270
  2.4 12.3 %collective-permute-start.1 = (bf16[2,96,1024]{2,1,0:T(8,128)(2,1)S(1)}, bf16[2,96,1024]{2,1,0:T(8,128)(2,1)S(1)}, u32[]{:S(2)}, u32[]{:S(2)}) collective-permute-start(bf16[2,96,1024]{2,1,0:T(8,128)(2,1)S(1)} %reshape.16.x_ref), channel_id=1, source_target_pairs={{0,32},{64,96},{128,160},{192,224},{32,0},{96,64},{160,128},{224,1... | collective-permute-start | bytes 1179656 | tf_op jit(solution)/shard_map/ppermute | solution.py:270
  6.2 8.6 %copy-start.2 = (bf16[2,96,1024]{2,1,0:T(8,128)(2,1)}, bf16[2,96,1024]{2,1,0:T(8,128)(2,1)S(1)}, u32[]{:S(2)}) copy-start(bf16[2,96,1024]{2,1,0:T(8,128)(2,1)S(1)} %collective-permute-done.xa_ref) | copy-start | bytes 1179652
  6.2 16.4 %copy-start.8 = (bf16[2,24,4,1024]{3,2,1,0:T(4,128)(2,1)S(1)}, bf16[2,24,4,1024]{3,2,1,0:T(4,128)(2,1)}, u32[]{:S(2)}) copy-start(bf16[2,24,4,1024]{3,2,1,0:T(4,128)(2,1)} %param.11) | copy-start | bytes 1179652
  14.7 0.8 copy-start.3
  15.4 24.8 %collective-permute-start.2 = (bf16[6,32,1024]{2,1,0:T(8,128)(2,1)S(1)}, bf16[6,32,1024]{2,1,0:T(8,128)(2,1)S(1)}, u32[]{:S(2)}, u32[]{:S(2)}) collective-permute-start(bf16[6,32,1024]{2,1,0:T(8,128)(2,1)S(1)} %get-tuple-element.41), channel_id=1, source_target_pairs={{0,1},{2,3},{4,5},{6,7},{8,9},{10,11},{12,13},{14,15},{16,17},{18,... | collective-permute-start | bytes 1179656 | tf_op jit(solution)/shard_map/ppermute | solution.py:270
  17.0 23.2 %collective-permute-start.3 = (bf16[6,32,1024]{2,1,0:T(8,128)(2,1)S(1)}, bf16[6,32,1024]{2,1,0:T(8,128)(2,1)S(1)}, u32[]{:S(2)}, u32[]{:S(2)}) collective-permute-start(bf16[6,32,1024]{2,1,0:T(8,128)(2,1)S(1)} %get-tuple-element.40), channel_id=1, source_target_pairs={{1,2},{3,4},{5,6},{7,8},{9,10},{11,12},{13,14},{15,16},{17,18},{19... | collective-permute-start | bytes 1179656 | tf_op jit(solution)/shard_map/ppermute | solution.py:270
  22.7 3.7 %copy-start.1 = (bf16[2,96,1024]{2,1,0:T(8,128)(2,1)}, bf16[2,96,1024]{2,1,0:T(8,128)(2,1)S(1)}, u32[]{:S(2)}) copy-start(bf16[2,96,1024]{2,1,0:T(8,128)(2,1)S(1)} %reshape.17.gr_ref) | copy-start | bytes 1179652
  22.8 48.6 %collective-permute-start.6 = (bf16[2,96,1024]{2,1,0:T(8,128)(2,1)S(1)}, bf16[2,96,1024]{2,1,0:T(8,128)(2,1)S(1)}, u32[]{:S(2)}, u32[]{:S(2)}) collective-permute-start(bf16[2,96,1024]{2,1,0:T(8,128)(2,1)S(1)} %reshape.17.gr_ref), channel_id=1, source_target_pairs={{32,64},{96,128},{160,192},{64,32},{128,96},{192,160},{33,65},{97,... | collective-permute-start | bytes 1179656 | tf_op jit(solution)/shard_map/ppermute | solution.py:270
  23.4 48.0 %collective-permute-start.7 = (bf16[2,96,1024]{2,1,0:T(8,128)(2,1)S(1)}, bf16[2,96,1024]{2,1,0:T(8,128)(2,1)S(1)}, u32[]{:S(2)}, u32[]{:S(2)}) collective-permute-start(bf16[2,96,1024]{2,1,0:T(8,128)(2,1)S(1)} %reshape.17.gr_ref), channel_id=1, source_target_pairs={{0,32},{64,96},{128,160},{192,224},{32,0},{96,64},{160,128},{224,1... | collective-permute-start | bytes 1179656 | tf_op jit(solution)/shard_map/ppermute | solution.py:270
  40.2 0.7 copy-start.4
  40.2 0.9 copy-start.5
  65.0 16.3 %collective-permute-start.4 = (f32[12,4,256]{2,1,0:T(4,128)}, f32[12,4,256]{2,1,0:T(4,128)S(1)}, u32[]{:S(2)}, u32[]{:S(2)}) collective-permute-start(f32[12,4,256]{2,1,0:T(4,128)} %get-tuple-element.30), channel_id=1, source_target_pairs={{32,64},{96,128},{160,192},{64,32},{128,96},{192,160},{33,65},{97,... | collective-permute-start | bytes 147464 | tf_op jit(solution)/shard_map/ppermute | solution.py:270
  65.6 15.6 %collective-permute-start.5 = (f32[12,4,256]{2,1,0:T(4,128)}, f32[12,4,256]{2,1,0:T(4,128)S(1)}, u32[]{:S(2)}, u32[]{:S(2)}) collective-permute-start(f32[12,4,256]{2,1,0:T(4,128)} %get-tuple-element.30), channel_id=1, source_target_pairs={{0,32},{64,96},{128,160},{192,224},{32,0},{96,64},{160,128},{224,1... | collective-permute-start | bytes 147464 | tf_op jit(solution)/shard_map/ppermute | solution.py:270
  71.4 0.7 copy-start.6
  72.1 0.7 copy-start.7
  81.2 0.6 copy-start.12
  81.3 0.6 copy-start.13
  81.9 18.5 %copy-start.9 = (bf16[2,96,1024]{2,1,0:T(8,128)(2,1)S(1)}, bf16[2,96,1024]{2,1,0:T(8,128)(2,1)}, u32[]{:S(2)}) copy-start(bf16[2,96,1024]{2,1,0:T(8,128)(2,1)} %get-tuple-element.29) | copy-start | bytes 1179652
  95.1 6.3 %collective-permute-start.8 = (bf16[2,32,1024]{2,1,0:T(8,128)(2,1)}, bf16[2,32,1024]{2,1,0:T(8,128)(2,1)S(1)}, u32[]{:S(2)}, u32[]{:S(2)}) collective-permute-start(bf16[2,32,1024]{2,1,0:T(8,128)(2,1)} %get-tuple-element.38), channel_id=1, source_target_pairs={{0,1},{2,3},{4,5},{6,7},{8,9},{10,11},{12,13},{14,15},{16,17},{18,... | collective-permute-start | bytes 393224 | tf_op jit(solution)/shard_map/ppermute | solution.py:270
  95.1 12.1 %collective-permute-start.9 = (bf16[2,32,1024]{2,1,0:T(8,128)(2,1)}, bf16[2,32,1024]{2,1,0:T(8,128)(2,1)S(1)}, u32[]{:S(2)}, u32[]{:S(2)}) collective-permute-start(bf16[2,32,1024]{2,1,0:T(8,128)(2,1)} %get-tuple-element.39), channel_id=1, source_target_pairs={{1,2},{3,4},{5,6},{7,8},{9,10},{11,12},{13,14},{15,16},{17,18},{19... | collective-permute-start | bytes 393224 | tf_op jit(solution)/shard_map/ppermute | solution.py:270
  101.3 5.9 %copy-start.10 = (bf16[2,32,1024]{2,1,0:T(8,128)(2,1)}, bf16[2,32,1024]{2,1,0:T(8,128)(2,1)S(1)}, u32[]{:S(2)}) copy-start(bf16[2,32,1024]{2,1,0:T(8,128)(2,1)S(1)} %collective-permute-done.8.re_ref) | copy-start | bytes 393220
  107.2 0.7 copy-start.11
where the time goes:
time: 112 us
  Pallas kernels  60.7 us (54%)
  starting transfers between devices  27.1 us (24%)
  waiting for transfers between devices  14.3 us (13%)
  local copies, waits for them, and re-layouts  8.38 us (7%)
    pallas_call x7, Pallas kernels, call(): pl.pallas_call(body, out_shape=[jax.ShapeDtypeStruct(s, d) for s, d in ou...  60.7 us
    ppermute x10, starting transfers between devices, swap(): return lax.ppermute(block, axis, swap_pairs(lax.axis_size(axis), first))  27.1 us
    ppermute x10, waiting for transfers between devices, swap(): return lax.ppermute(block, axis, swap_pairs(lax.axis_size(axis), first))  14.3 us
    unnamed x30, local copies, waits for them, and re-layouts  4.31 us
    reshape x2, local copies, waits for them, and re-layouts, shards(): return (attended.reshape(inputs.shape), grad_in.reshape(inputs.shape))  2.78 us
  transfers between devices with their start and end apart: 10, of which 2 were waited for; matrix products, arithmetic and copies ran while one was open for 1% of the time, Pallas kernels for 41%

commit v1 on v0

v1 whole, which is shorter than its diff:
```python
import functools

import jax
import jax.numpy as jnp
from jax import lax
from jax.experimental import pallas as pl
from jax.experimental.pallas import tpu as pltpu
from jax.sharding import PartitionSpec as P

HD = 64
RT = 2
RH = 7
BR = 8
WC = 4
GW = 256
HALF = BR * WC
PER = 4
VMEM_LIMIT = 28 * 1024 * 1024
NEG = -1e30
F32 = jnp.float32
BF16 = jnp.bfloat16


def nn(a, b):
    return lax.dot_general(a, b, (((1,), (0,)), ((), ())), preferred_element_type=F32)


def nt(a, b):
    return lax.dot_general(a, b, (((1,), (1,)), ((), ())), preferred_element_type=F32)


def tn(a, b):
    return lax.dot_general(a, b, (((0,), (0,)), ((), ())), preferred_element_type=F32)


def call(body, out_shapes, *args, places=None, scratch=(), limit=VMEM_LIMIT):
    places = places or {}
    return pl.pallas_call(
        body,
        out_shape=[jax.ShapeDtypeStruct(s, d) for s, d in out_shapes],
        in_specs=[pl.BlockSpec(memory_space=places.get(i, pltpu.VMEM)) for i in range(len(args))],
        out_specs=[pl.BlockSpec(memory_space=pltpu.VMEM) for _ in out_shapes],
        scratch_shapes=list(scratch),
        compiler_params=pltpu.CompilerParams(vmem_limit_bytes=limit),
    )(*args)


def store_blocks(y, out_ref, g):
    frames, blocks, half, _ = y.shape
    for b in range(blocks):
        for f in range(frames):
            at = slice((f % 2) * half, (f % 2 + 1) * half)
            if len(out_ref.shape) == 4:
                out_ref[g, b, at, :] = y[f, b]
            else:
                out_ref[g, f // 2, b, at, :] = y[f, b]


def project(x, w_ref, out_ref, scale=None):
    for g in range(out_ref.shape[0]):
        y = nn(x, w_ref[:, g * GW : (g + 1) * GW])
        if scale is not None:
            y = y * scale
        store_blocks(y.astype(BF16).reshape(-1, 3, HALF, GW), out_ref, g)


def project_t(x, w_ref, out_ref):
    for g in range(out_ref.shape[0]):
        y = nt(x, w_ref[g * GW : (g + 1) * GW, :])
        store_blocks(y.astype(BF16).reshape(-1, 3, HALF, GW), out_ref, g)


def flat(ref):
    return ref[...].reshape(-1, ref.shape[-1])


def own_kernel(
    n_frames, n_rows, frames, rows,
    info_ref, x_ref, gr_ref, wq_hbm, wk_hbm, wv_hbm, wo_hbm,
    q_ref, k_ref, v_ref, ga_ref, wq_ref, wk_ref, wv_ref, wo_ref, fb_ref, bb_ref,
    sem,
):
    pairs = ((wk_hbm, wk_ref), (wv_hbm, wv_ref), (wq_hbm, wq_ref), (wo_hbm, wo_ref))
    copies = [pltpu.make_async_copy(src, dst, sem.at[i]) for i, (src, dst) in enumerate(pairs)]
    for c in copies:
        c.start()
    tm, h = info_ref[0], info_ref[1]
    off_a, off_b = slot_offsets(tm)
    offsets = (off_a, off_a + 1, 0, 1, off_b, off_b + 1)
    for rb in range(3):
        for j in range(3):
            base = row_bias(rb, j, h, n_rows, rows)
            for s in range(6):
                at = (j * 6 + s) * HALF
                fb_ref[rb, at : at + HALF] = base + frame_bias(offsets[s], 0, tm, n_frames, frames)
            for p, off in enumerate((off_a, off_b)):
                for f in range(2):
                    at = (j * 2 + f) * HALF
                    bb_ref[p, rb, at : at + HALF] = base + frame_bias(f, off, tm, n_frames, frames)
    x = flat(x_ref)
    copies[0].wait()
    project(x, wk_ref, k_ref)
    copies[1].wait()
    project(x, wv_ref, v_ref)
    copies[2].wait()
    project(x, wq_ref, q_ref, HD**-0.5)
    copies[3].wait()
    project_t(flat(gr_ref), wo_ref, ga_ref)


def edge_kernel(for_odd, info_ref, x_ref, xa_ref, xb_ref, after_ref, out_ref):
    for parity in range(2):

        @pl.when(info_ref[1] % 2 == parity)
        def _(start=2 * HALF * (parity if for_odd else 1 - parity)):
            for s, ref in enumerate((xa_ref, x_ref, xb_ref)):
                out_ref[2 * s : 2 * s + 2] = ref[:, start : start + HALF]


def side_kernel(xa_ref, xb_ref, wq_ref, wk_ref, wv_ref, after_ref, q_ref, k_ref, v_ref):
    x = jnp.concatenate([flat(xa_ref), flat(xb_ref)], axis=0)
    project(x, wk_ref, k_ref)
    project(x, wv_ref, v_ref)
    project(x, wq_ref, q_ref, HD**-0.5)


def side_grad_kernel(ga_ref, gb_ref, wo_ref, after_ref, out_ref):
    project_t(jnp.concatenate([flat(ga_ref), flat(gb_ref)], axis=0), wo_ref, out_ref)


def spread(block):
    heads = block.shape[1] // HD
    lane = lax.broadcasted_iota(jnp.int32, block.shape, 1) // HD
    zero = jnp.zeros_like(block)
    return jnp.concatenate([jnp.where(lane == h, block, zero) for h in range(heads)], axis=0)


def row_bias(rb, j, h, n_rows, rows):
    w = j * BR + lax.broadcasted_iota(jnp.int32, (HALF, GW), 0) // WC
    r = (lax.broadcasted_iota(jnp.int32, (HALF, GW), 1) % HALF) // WC
    diff = w - r - BR
    glob = h * rows + rb * BR + w - BR
    ok = (diff >= -RH) & (diff <= RH) & (glob >= 0) & (glob < n_rows)
    return jnp.where(ok, F32(0), F32(NEG))


def frame_bias(key_off, query_off, tm, n_frames, frames):
    fq = (lax.broadcasted_iota(jnp.int32, (1, GW), 1) // HALF) % 2 + query_off
    diff = key_off - fq
    glob = tm * frames + key_off
    ok = (diff >= -RT) & (diff <= RT) & (glob >= 0) & (glob < n_frames)
    return jnp.where(ok, F32(0), F32(NEG))


def slot_offsets(tm):
    odd = tm % 2
    return 4 * odd - 2, 2 - 4 * odd


def pipeline(count, *stages):
    held = {}
    for t in range(count + len(stages) - 1):
        for s, stage in enumerate(stages):
            u = t - s
            if 0 <= u < count:
                held[u] = stage(u, held.get(u))


def forward_kernel(
    info_ref, xe_ref, xo_ref, wk_ref, wv_ref, q_ref, ga_ref, k_ref, v_ref, ks_ref, vs_ref, bias_ref, after_ref,
    stats_ref, mixed_ref, dq_ref, dk_ref, dv_ref, krow_ref, vrow_ref,
    kh_ref, vh_ref,
):
    groups = q_ref.shape[0]
    own = slice(2 * HALF, 4 * HALF)
    h_odd = info_ref[1] % 2
    for x_ref, side in ((xe_ref, 1 - h_odd), (xo_ref, h_odd)):
        x = flat(x_ref)
        for g in range(groups):
            kh_ref[side, g] = nn(x, wk_ref[:, g * GW : (g + 1) * GW]).astype(BF16)
            vh_ref[side, g] = nn(x, wv_ref[:, g * GW : (g + 1) * GW]).astype(BF16)
    for side in range(2):
        for g in range(groups):
            krow_ref[side, g] = kh_ref[side, g, own]
            vrow_ref[side, g] = vh_ref[side, g, own]
    dk_ref[...] = jnp.zeros_like(dk_ref)
    dv_ref[...] = jnp.zeros_like(dv_ref)
    diag = (
        lax.broadcasted_iota(jnp.int32, (GW, GW), 0) // HD == lax.broadcasted_iota(jnp.int32, (GW, GW), 1) // 64
    )

    def some(i, carry):
        cache = {}

        def blocks(g, which, margin_ref, side_ref, own_ref):
            if (g, which) not in cache:
                at = i * PER + g
                mid = [jnp.concatenate([side_ref[at, 0, b], own_ref[at, b], side_ref[at, 1, b]], axis=0) for b in range(3)]
                cache[g, which] = [margin_ref[0, at], *mid, margin_ref[1, at]]
            return cache[g, which]

        def flipped(g, which, b, block):
            if (g, which, b) not in cache:
                cache[g, which, b] = block.T
            return cache[g, which, b]

        def scores(u, _):
            g, rb = u // 3, u % 3
            kb = blocks(g, 0, kh_ref, ks_ref, k_ref)[rb : rb + 3]
            vb = blocks(g, 1, vh_ref, vs_ref, v_ref)[rb : rb + 3]
            kt = [flipped(g, 0, rb + j, kb[j]) for j in range(3)]
            vt = [flipped(g, 1, rb + j, vb[j]) for j in range(3)]
            qs, gs = spread(q_ref[i * PER + g, rb]), spread(ga_ref[i * PER + g, rb])
            s = nt(jnp.concatenate(kb, axis=0), qs)
            dp = nt(jnp.concatenate(vb, axis=0), gs)
            return kt, vt, qs, gs, s, dp

        def soft(u, held):
            rb = u % 3
            kt, vt, qs, gs, s, dp = held
            s = s + bias_ref[rb]
            m = jnp.max(s, axis=0, keepdims=True)
            e = jnp.exp(s - m)
            rl = 1.0 / jnp.sum(e, axis=0, keepdims=True)
            delta = jnp.sum(e * dp, axis=0, keepdims=True) * rl
            p = e * rl
            row = i * (3 * PER) + u
            stats_ref[row, 0:1, :] = m
            stats_ref[row, 1:2, :] = rl
            stats_ref[row, 2:3, :] = delta
            stats_ref[row, 3:4, :] = delta
            return kt, vt, qs, gs, p.astype(BF16), (p * (dp - delta)).astype(BF16)

        def back(u, held):
            g, rb = i * PER + u // 3, u % 3
            kt, vt, qs, gs, pb, ds = held

            def gather(t, p):
                parts = [nn(t[j], p[j * 6 * HALF : (j + 1) * 6 * HALF]) for j in range(3)]
                return parts[0] + parts[1] + parts[2]

            def fold(y):
                y = jnp.where(diag, y, 0.0)
                y = (y[:, : GW // 2] + y[:, GW // 2 :]).astype(BF16).T
                return y[:64] + y[64:]

            mixed_ref[g, rb] = fold(gather(vt, pb))
            dq_ref[g, rb] = fold(gather(kt, ds) * (HD**-0.5))

            def middle(p):
                return jnp.concatenate([p[(j * 6 + 2) * HALF : (j * 6 + 4) * HALF] for j in range(3)], axis=0)

            dk_ref[g, rb : rb + 3] += nn(middle(ds), qs).reshape(3, 2 * HALF, GW)
            dv_ref[g, rb : rb + 3] += nn(middle(pb), gs).reshape(3, 2 * HALF, GW)

        pipeline(3 * PER, scores, soft, back)
        return carry

    lax.fori_loop(0, groups // PER, some, 0)


def unblock(y, out_ref):
    for b in range(3):
        for f in range(out_ref.shape[0]):
            part = y[b, f * HALF : (f + 1) * HALF].astype(out_ref.dtype)
            if len(out_ref.shape) == 3:
                out_ref[f, b * HALF : (b + 1) * HALF, :] = part
            else:
                out_ref[f, b * BR : (b + 1) * BR] = part.reshape(BR, WC, -1)


def middle_kernel(mixed_ref, dq_ref, wo_ref, wq_ref, att_ref, dxq_ref):
    groups = mixed_ref.shape[0]
    mixed = jnp.concatenate([flat(mixed_ref.at[g]) for g in range(groups)], axis=1)
    unblock(nn(mixed, wo_ref[...]).reshape(3, 2 * HALF, -1), att_ref)
    dq = jnp.concatenate([flat(dq_ref.at[g]) for g in range(groups)], axis=1)
    dxq_ref[...] = nt(dq, wq_ref[...]).reshape(dxq_ref.shape)


def margin_kernel(
    info_ref, sa_ref, sb_ref, qs_ref, gs_ref, krow_ref, vrow_ref, dk_ref, dv_ref, bias_ref, wk_ref, wv_ref, after_ref,
    me_ref, mo_ref,
    dka_ref, dva_ref, edge_ref,
):
    groups = qs_ref.shape[0]
    parts = {}

    def scores(u, _):
        g, side, p = u // 4, u // 2 % 2, u % 2
        qs, gs = spread(qs_ref[g, p, 2 * side]), spread(gs_ref[g, p, 2 * side])
        return qs, gs, nt(krow_ref[side, g], qs), nt(vrow_ref[side, g], gs)

    def soft(u, held):
        g, side, p = u // 4, u // 2 % 2, u % 2
        qs, gs, s, dp = held
        stat_ref, row = (sa_ref, sb_ref)[p], g * 3 + 2 * side
        m, rl, delta = stat_ref[row, 0:1, :], stat_ref[row, 1:2, :], stat_ref[row, 2:3, :]
        at = 4 * side * HALF
        pr = jnp.exp(s + bias_ref[p, 2 * side, at : at + 2 * HALF] - m) * rl
        return qs, gs, (pr * (dp - delta)).astype(BF16), pr.astype(BF16)

    def back(u, held):
        qs, gs, ds, pb = held
        parts[u] = nn(ds, qs), nn(pb, gs)

    pipeline(4 * groups, scores, soft, back)
    for g in range(groups):
        for side in range(2):
            u = 4 * g + 2 * side
            dka_ref[g, side] = (dk_ref[g, 4 * side] + parts[u][0] + parts[u + 1][0]).astype(BF16)
            dva_ref[g, side] = (dv_ref[g, 4 * side] + parts[u][1] + parts[u + 1][1]).astype(BF16)
    dk = jnp.concatenate([flat(dka_ref.at[g]) for g in range(groups)], axis=1)
    dv = jnp.concatenate([flat(dva_ref.at[g]) for g in range(groups)], axis=1)
    dx = (nt(dk, wk_ref[...]) + nt(dv, wv_ref[...])).astype(BF16)
    edge_ref[...] = dx.reshape(edge_ref.shape)
    h_odd = info_ref[1] % 2
    me_ref[...] = edge_ref[1 - h_odd]
    mo_ref[...] = edge_ref[h_odd]


def backward_kernel(
    sa_ref, sb_ref, qs_ref, gs_ref, k_ref, v_ref, dk_ref, dv_ref, dxq_ref, bias_ref, wk_ref, wv_ref,
    own_ref,
    dka_ref, dva_ref,
):
    groups = k_ref.shape[0]
    dka_ref[...] = dk_ref[:, 1:4]
    dva_ref[...] = dv_ref[:, 1:4]
    reach = ((0, 2, 2 * HALF), (0, 3, 0), (1, 3, 0))

    def group(g, carry):
        def scores(u, _):
            rb, p = u // 2, u % 2
            lo, hi, _ = reach[rb]
            qs, gs = spread(qs_ref[g, p, rb]), spread(gs_ref[g, p, rb])
            return qs, gs, nt(flat(k_ref.at[g, lo:hi]), qs), nt(flat(v_ref.at[g, lo:hi]), gs)

        def soft(u, held):
            rb, p = u // 2, u % 2
            qs, gs, s, dp = held
            stat_ref, row, at = (sa_ref, sb_ref)[p], g * 3 + rb, reach[rb][2]
            m, rl, delta = stat_ref[row, 0:1, :], stat_ref[row, 1:2, :], stat_ref[row, 2:3, :]
            pr = jnp.exp(s + bias_ref[p, rb, at : at + s.shape[0]] - m) * rl
            return qs, gs, pr.astype(BF16), (pr * (dp - delta)).astype(BF16)

        def back(u, held):
            lo, hi, _ = reach[u // 2]
            qs, gs, pb, ds = held
            dka_ref[g, lo:hi] += nn(ds, qs).reshape(hi - lo, 2 * HALF, GW)
            dva_ref[g, lo:hi] += nn(pb, gs).reshape(hi - lo, 2 * HALF, GW)

        pipeline(6, scores, soft, back)
        return carry

    lax.fori_loop(0, groups, group, 0)
    dk = jnp.concatenate([flat(dka_ref.at[g]).astype(BF16) for g in range(groups)], axis=1)
    dv = jnp.concatenate([flat(dva_ref.at[g]).astype(BF16) for g in range(groups)], axis=1)
    dx = (nt(dk, wk_ref[...]) + nt(dv, wv_ref[...])).reshape(3, 2 * HALF, -1)
    unblock(dx + dxq_ref[...], own_ref)


def last_kernel(info_ref, own_ref, re_ref, ro_ref, out_ref, acc_ref):
    h_odd = info_ref[1] % 2
    top, bottom = slice(0, HALF), slice(2 * HALF, 3 * HALF)
    acc_ref[...] = own_ref[...]
    for parity, of_even, of_odd in ((0, bottom, top), (1, top, bottom)):

        @pl.when(h_odd == parity)
        def _(of_even=of_even, of_odd=of_odd):
            acc_ref[:, of_even] += re_ref[...].astype(F32)
            acc_ref[:, of_odd] += ro_ref[...].astype(F32)

    out_ref[...] = acc_ref[...].astype(BF16).reshape(out_ref.shape)


def swap_pairs(count, first):
    pairs = [(i, i + 1) for i in range(first, count - 1, 2)]
    return pairs + [(b, a) for a, b in pairs]


def swap(block, axis, first):
    return lax.ppermute(block, axis, swap_pairs(lax.axis_size(axis), first))


def shards(inputs, w_query, w_key, w_value, w_out, grad_out):
    frames, rows, cols, width = inputs.shape
    groups = width // GW
    tokens = rows * cols
    tm, h = lax.axis_index("tm"), lax.axis_index("height")
    n_frames, n_rows = lax.axis_size("tm") * frames, lax.axis_size("height") * rows
    info = jnp.stack([tm, h]).astype(jnp.int32)
    dims = (n_frames, n_rows, frames, rows)

    x = inputs.reshape(frames, tokens, width)
    xa = swap(x, "tm", 1)
    xb = swap(x, "tm", 0)
    grad = grad_out.reshape(frames, tokens, width)
    ga = swap(grad, "tm", 1)
    gb = swap(grad, "tm", 0)

    own_shape = ((groups, 3, 2 * HALF, GW), BF16)
    side_shape = ((groups, 2, 3, 2 * HALF, GW), BF16)
    weight_shape = (w_query.shape, BF16)
    hbm = {i: pltpu.HBM for i in range(3, 7)}
    q, k, v, ga_own, wq, wk, wv, wo, f_bias, b_bias = call(
        functools.partial(own_kernel, *dims),
        [own_shape] * 4 + [weight_shape] * 4 + [((3, 18 * HALF, GW), F32), ((2, 3, 6 * HALF, GW), F32)],
        info, x, grad, w_query, w_key, w_value, w_out,
        places={0: pltpu.SMEM, **hbm},
        scratch=[pltpu.SemaphoreType.DMA((4,))],
        limit=41 * 1024 * 1024,
    )
    margin_shape = ((3 * frames, HALF, width), BF16)
    places = {0: pltpu.SMEM, 4: pl.ANY}
    (edge,) = call(functools.partial(edge_kernel, True), [margin_shape], info, x, xa, xb, q, places=places)
    xo = swap(edge, "height", 1)
    q_side, k_side, v_side = call(
        side_kernel, [side_shape] * 3, xa, xb, wq, wk, wv, edge, places={5: pl.ANY}
    )
    (edge,) = call(functools.partial(edge_kernel, False), [margin_shape], info, x, xa, xb, k_side, places=places)
    xe = swap(edge, "height", 0)
    (ga_side,) = call(side_grad_kernel, [side_shape], ga, gb, wo, edge, places={3: pl.ANY})

    acc_shape = (groups, 5, 2 * HALF, GW)
    row_shape = ((2, groups, 2 * HALF, GW), BF16)
    stats, mixed, dq, dk, dv, k_row, v_row = call(
        forward_kernel,
        [((3 * groups, 4, GW), F32), own_shape, own_shape, (acc_shape, F32), (acc_shape, F32), row_shape, row_shape],
        info, xe, xo, wk, wv, q, ga_own, k, v, k_side, v_side, f_bias, ga_side,
        places={0: pltpu.SMEM, 12: pl.ANY},
        scratch=[pltpu.VMEM((2, groups, 6 * HALF, GW), BF16)] * 2,
    )
    sa = swap(stats, "tm", 1)
    sb = swap(stats, "tm", 0)
    token_shape = (frames, tokens, width)
    attended, dxq = call(middle_kernel, [(inputs.shape, BF16), ((3, 2 * HALF, width), F32)], mixed, dq, wo, wq)
    edge_shape = (frames, HALF, width)
    me, mo = call(
        margin_kernel,
        [(edge_shape, BF16)] * 2,
        info, sa, sb, q_side, ga_side, k_row, v_row, dk, dv, b_bias, wk, wv, dxq,
        places={0: pltpu.SMEM, 12: pl.ANY},
        scratch=[pltpu.VMEM((groups, 2, 2 * HALF, GW), BF16)] * 2 + [pltpu.VMEM((2, *edge_shape), BF16)],
    )
    ro = swap(mo, "height", 1)
    re = swap(me, "height", 0)
    (own,) = call(
        backward_kernel,
        [(token_shape, F32)],
        sa, sb, q_side, ga_side, k, v, dk, dv, dxq, b_bias, wk, wv,
        scratch=[pltpu.VMEM((groups, 3, 2 * HALF, GW), F32)] * 2,
    )
    (grad_in,) = call(
        last_kernel, [(inputs.shape, BF16)], info, own, re, ro,
        places={0: pltpu.SMEM}, scratch=[pltpu.VMEM(token_shape, F32)],
    )
    return (attended, grad_in)


def solution(mesh):
    placed = (P("tm", "height", None, None), P(), P(), P(), P(), P("tm", "height", None, None))
    return jax.shard_map(
        shards,
        mesh=mesh,
        in_specs=placed,
        out_specs=(P("tm", "height", None, None), P("tm", "height", None, None)),
        check_vma=False,
    )
```

time: 112 us -> 72.2 us (0.64)
  the two profiles are of different devices: /device:TPU:89 before, /device:TPU:95 now
where the time goes in v1:
time: 72.2 us; the launch traced here: 71.9 us
  starting transfers between devices  33.7 us (47%)
  Pallas kernels  32.9 us (46%)
  local copies, waits for them, and re-layouts  2.86 us (4%)
  waiting for transfers between devices  1.55 us (2%)
  between operations  0.82 us (1%)
    ppermute x10, starting transfers between devices, swap(): return lax.ppermute(block, axis, swap_pairs(lax.axis_size(axis), first))  33.7 us
    pallas_call x10, Pallas kernels, call(): pl.pallas_call(body, out_shape=[jax.ShapeDtypeStruct(s, d) for s, d in ou...  32.9 us
    ppermute x10, waiting for transfers between devices, swap(): return lax.ppermute(block, axis, swap_pairs(lax.axis_size(axis), first))  1.55 us
  transfers between devices with their start and end apart: 10, of which 2 were waited for; matrix products, arithmetic and copies ran while one was open for 2% of the time, Pallas kernels for 24%

profile of v1, /device:TPU:95, one launch (start us, length us, event | category | flops | bytes accessed | tf_op | source)
XLA Modules:
  0.0 71.9 jit_solution(17836353169295351440)
XLA Ops:
  0.6 1.1 %reshape.10.x_ref = bf16[2,96,1024]{2,1,0:T(8,128)(2,1)S(1)} reshape(bf16[2,24,4,1024]{3,2,1,0:T(4,128)(2,1)} %param.6) | data formatting | bytes 786432 | tf_op jit(solution)/shard_map/reshape | solution.py:394
  1.7 0.6 collective-permute-start.1
  2.4 4.1 %collective-permute-start = (bf16[2,96,1024]{2,1,0:T(8,128)(2,1)S(1)}, bf16[2,96,1024]{2,1,0:T(8,128)(2,1)S(1)}, u32[]{:S(2)}, u32[]{:S(2)}) collective-permute-start(bf16[2,96,1024]{2,1,0:T(8,128)(2,1)S(1)} %reshape.10.x_ref), channel_id=1, source_target_pairs={{32,64},{96,128},{160,192},{64,32},{128,96},{192,160},{33,65},{97,... | collective-permute-start | bytes 1179656 | tf_op jit(solution)/shard_map/ppermute | solution.py:382
  6.5 1.1 %reshape.11.gr_ref = bf16[2,96,1024]{2,1,0:T(8,128)(2,1)S(1)} reshape(bf16[2,24,4,1024]{3,2,1,0:T(4,128)(2,1)} %param.11) | data formatting | bytes 786432 | tf_op jit(solution)/shard_map/reshape | solution.py:397
  7.6 0.1 collective-permute-start.5
  7.7 4.0 %collective-permute-start.4 = (bf16[2,96,1024]{2,1,0:T(8,128)(2,1)S(1)}, bf16[2,96,1024]{2,1,0:T(8,128)(2,1)S(1)}, u32[]{:S(2)}, u32[]{:S(2)}) collective-permute-start(bf16[2,96,1024]{2,1,0:T(8,128)(2,1)S(1)} %reshape.11.gr_ref), channel_id=1, source_target_pairs={{32,64},{96,128},{160,192},{64,32},{128,96},{192,160},{33,65},{97,... | collective-permute-start | bytes 1179656 | tf_op jit(solution)/shard_map/ppermute | solution.py:382
  11.7 0.1 pad_add_fusion.info_ref
  11.8 5.4 %shard_map.77 = (bf16[4,3,64,256]{3,2,1,0:T(8,128)(2,1)S(1)}, bf16[4,3,64,256]{3,2,1,0:T(8,128)(2,1)S(1)}, bf16[4,3,64,256]{3,2,1,0:T(8,128)(2,1)S(1)}, bf16[4,3...) custom-call(s32[2]{0:T(128)S(1)} %pad_add_fusion.info_ref, ...), custom_call_target="tpu_custom_call" | custom-call | tf_op jit(solution)/shard_map/pallas_call | solution.py:38
  17.1 0.0 collective-permute-done.1.xb_ref
  17.2 0.0 collective-permute-done.xa_ref
  17.2 0.6 shard_map.78.after_ref
  17.8 7.8 %collective-permute-start.3 = (bf16[6,32,1024]{2,1,0:T(8,128)(2,1)S(1)}, bf16[6,32,1024]{2,1,0:T(8,128)(2,1)S(1)}, u32[]{:S(2)}, u32[]{:S(2)}) collective-permute-start(bf16[6,32,1024]{2,1,0:T(8,128)(2,1)S(1)} %shard_map.78.after_ref), channel_id=1, source_target_pairs={{1,2},{3,4},{5,6},{7,8},{9,10},{11,12},{13,14},{15,16},{17,18},{19... | collective-permute-start | bytes 1179656 | tf_op jit(solution)/shard_map/ppermute | solution.py:382
  25.6 2.6 %shard_map.79 = (bf16[4,2,3,64,256]{4,3,2,1,0:T(8,128)(2,1)S(1)}, bf16[4,2,3,64,256]{4,3,2,1,0:T(8,128)(2,1)S(1)}, bf16[4,2,3,64,256]{4,3,2,1,0:T(8,128)(2,1)S(1)}) custom-call(bf16[2,96,1024]{2,1,0:T(8,128)(2,1)S(1)} %collective-permute-done.xa_ref, bf16[2,96,1024]{2,1,0:T(8,128)(2,1)S(1)} %collective-permute-done.1.xb_ref, ...), custom_call_target="tpu_custom_call" | custom-call | tf_op jit(solution)/shard_map/pallas_call | solution.py:38
  28.2 0.6 shard_map.80.after_ref
  28.8 0.3 collective-permute-start.2
  29.1 0.0 collective-permute-done.5.gb_ref
  29.1 0.7 copy-done
  29.8 1.0 %shard_map.81.after_ref.gs_ref = bf16[4,2,3,64,256]{4,3,2,1,0:T(8,128)(2,1)S(1)} custom-call(bf16[2,96,1024]{2,1,0:T(8,128)(2,1)S(1)} %collective-permute-done.4.ga_ref, bf16[2,96,1024]{2,1,0:T(8,128)(2,1)S(1)} %collective-permute-done.5.gb_ref, bf16[1024,1024]{1,0:T(8,128)(2,1)S(1)} %copy-done, bf16[6,32,1024]{2,1,0:T(8,128)(2,1)S(1)} %shard_map.80.after_ref), custom_call_target="tpu_custom_call" | custom-call | tf_op jit(solution)/shard_map/pallas_call | solution.py:38
  30.8 1.4 %collective-permute-done.3.xo_ref = bf16[6,32,1024]{2,1,0:T(8,128)(2,1)S(1)} collective-permute-done((bf16[6,32,1024]{2,1,0:T(8,128)(2,1)S(1)}, bf16[6,32,1024]{2,1,0:T(8,128)(2,1)S(1)}, u32[]{:S(2)}, u32[]{:S(2)}) %collective-permute-start.3) | collective-permute-done | bytes 393248 | tf_op jit(solution)/shard_map/ppermute | solution.py:382
  32.2 0.0 collective-permute-done.2.xe_ref
  32.2 9.7 %shard_map.82 = (f32[12,4,256]{2,1,0:T(4,128)S(1)}, bf16[4,3,64,256]{3,2,1,0:T(8,128)(2,1)S(1)}, bf16[4,3,64,256]{3,2,1,0:T(8,128)(2,1)S(1)}, f32[4,5,64,256]{3,...) custom-call(s32[2]{0:T(128)S(1)} %pad_add_fusion.info_ref, ...), custom_call_target="tpu_custom_call" | custom-call | tf_op jit(solution)/shard_map/pallas_call | solution.py:38
  42.0 2.5 %collective-permute-start.7 = (f32[12,4,256]{2,1,0:T(4,128)S(1)}, f32[12,4,256]{2,1,0:T(4,128)S(1)}, u32[]{:S(2)}, u32[]{:S(2)}) collective-permute-start(f32[12,4,256]{2,1,0:T(4,128)S(1)} %get-tuple-element.40), channel_id=1, source_target_pairs={{0,32},{64,96},{128,160},{192,224},{32,0},{96,64},{160,128},{224,1... | collective-permute-start | bytes 147464 | tf_op jit(solution)/shard_map/ppermute | solution.py:382
  44.5 5.4 %collective-permute-start.6 = (f32[12,4,256]{2,1,0:T(4,128)S(1)}, f32[12,4,256]{2,1,0:T(4,128)S(1)}, u32[]{:S(2)}, u32[]{:S(2)}) collective-permute-start(f32[12,4,256]{2,1,0:T(4,128)S(1)} %get-tuple-element.40), channel_id=1, source_target_pairs={{32,64},{96,128},{160,192},{64,32},{128,96},{192,160},{33,65},{97,... | collective-permute-start | bytes 147464 | tf_op jit(solution)/shard_map/ppermute | solution.py:382
  49.9 1.4 %shard_map.83 = (bf16[2,24,4,1024]{3,2,1,0:T(4,128)(2,1)}, f32[3,64,1024]{2,1,0:T(8,128)S(1)}) custom-call(bf16[4,3,64,256]{3,2,1,0:T(8,128)(2,1)S(1)} %get-tuple-element.37.mixed_ref, bf16[4,3,64,256]{3,2,1,0:T(8,128)(2,1)S(1)} %get-tuple-element.38.dq_ref, bf16[1024,1024]{1,0:T(8,128)(2,1)S(1)} %copy-done, bf16[1024,1024]{1,0:T(8,128)(2,1)S(1)} %get-tuple-element.26.wq_ref), custom_call_target="tpu_custom_call" | custom-call | tf_op jit(solution)/shard_map/pallas_call | solution.py:38
  51.3 0.0 collective-permute-done.7.sb_ref
  51.3 0.1 collective-permute-done.6.sa_ref
  51.4 4.2 %shard_map.85 = (bf16[2,32,1024]{2,1,0:T(8,128)(2,1)S(1)}, bf16[2,32,1024]{2,1,0:T(8,128)(2,1)S(1)}) custom-call(s32[2]{0:T(128)S(1)} %pad_add_fusion.info_ref, f32[12,4,256]{2,1,0:T(4,128)S(1)} %collective-permute-done.6.sa_ref, f32[12,4,256]{2,1,0:T(4,128)S(1)} %collective-permute-done.7.sb_ref, bf16[4,2,3,64,256]{4,3,2,1,0:T(8,128)(2,1)S(1)} %get-tuple-element.41.qs_ref, ...), custom_call_target="tpu_custom_call" | custom-call | tf_op jit(solution)/shard_map/pallas_call | solution.py:38
  55.6 0.1 collective-permute-start.8
  55.7 8.7 %collective-permute-start.9 = (bf16[2,32,1024]{2,1,0:T(8,128)(2,1)S(1)}, bf16[2,32,1024]{2,1,0:T(8,128)(2,1)S(1)}, u32[]{:S(2)}, u32[]{:S(2)}) collective-permute-start(bf16[2,32,1024]{2,1,0:T(8,128)(2,1)S(1)} %get-tuple-element.49), channel_id=1, source_target_pairs={{1,2},{3,4},{5,6},{7,8},{9,10},{11,12},{13,14},{15,16},{17,18},{19... | collective-permute-start | bytes 393224 | tf_op jit(solution)/shard_map/ppermute | solution.py:382
  64.5 6.0 %shard_map.84.own_ref = f32[2,96,1024]{2,1,0:T(8,128)S(1)} custom-call(f32[12,4,256]{2,1,0:T(4,128)S(1)} %collective-permute-done.6.sa_ref, f32[12,4,256]{2,1,0:T(4,128)S(1)} %collective-permute-done.7.sb_ref, bf16[4,2,3,64,256]{4,3,2,1,0:T(8,128)(2,1)S(1)} %get-tuple-element.41.qs_ref, bf16[4,2,3,64,256]{4,3,2,1,0:T(8,128)(2,1)S(1)} %shard_map.81.after_ref.gs_ref, ...), custom_call_target="tpu_custom_call" | custom-call | tf_op jit(solution)/shard_map/pallas_call | solution.py:38
  70.4 0.0 collective-permute-done.8.re_ref
  70.5 1.4 %shard_map.86 = bf16[2,24,4,1024]{3,2,1,0:T(4,128)(2,1)} custom-call(s32[2]{0:T(128)S(1)} %pad_add_fusion.info_ref, f32[2,96,1024]{2,1,0:T(8,128)S(1)} %shard_map.84.own_ref, bf16[2,32,1024]{2,1,0:T(8,128)(2,1)S(1)} %collective-permute-done.8.re_ref, bf16[2,32,1024]{2,1,0:T(8,128)(2,1)S(1)} %collective-permute-done.9.ro_ref), custom_call_target="tpu_custom_call" | custom-call | tf_op jit(solution)/shard_map/pallas_call | solution.py:38
  (3 shorter events, 0.0 us)
Async XLA Ops:
  1.7 15.4 %collective-permute-start.1 = (bf16[2,96,1024]{2,1,0:T(8,128)(2,1)S(1)}, bf16[2,96,1024]{2,1,0:T(8,128)(2,1)S(1)}, u32[]{:S(2)}, u32[]{:S(2)}) collective-permute-start(bf16[2,96,1024]{2,1,0:T(8,128)(2,1)S(1)} %reshape.10.x_ref), channel_id=1, source_target_pairs={{0,32},{64,96},{128,160},{192,224},{32,0},{96,64},{160,128},{224,1... | collective-permute-start | bytes 1179656 | tf_op jit(solution)/shard_map/ppermute | solution.py:382
  2.4 14.8 %collective-permute-start = (bf16[2,96,1024]{2,1,0:T(8,128)(2,1)S(1)}, bf16[2,96,1024]{2,1,0:T(8,128)(2,1)S(1)}, u32[]{:S(2)}, u32[]{:S(2)}) collective-permute-start(bf16[2,96,1024]{2,1,0:T(8,128)(2,1)S(1)} %reshape.10.x_ref), channel_id=1, source_target_pairs={{32,64},{96,128},{160,192},{64,32},{128,96},{192,160},{33,65},{97,... | collective-permute-start | bytes 1179656 | tf_op jit(solution)/shard_map/ppermute | solution.py:382
  7.6 21.6 %collective-permute-start.5 = (bf16[2,96,1024]{2,1,0:T(8,128)(2,1)S(1)}, bf16[2,96,1024]{2,1,0:T(8,128)(2,1)S(1)}, u32[]{:S(2)}, u32[]{:S(2)}) collective-permute-start(bf16[2,96,1024]{2,1,0:T(8,128)(2,1)S(1)} %reshape.11.gr_ref), channel_id=1, source_target_pairs={{0,32},{64,96},{128,160},{192,224},{32,0},{96,64},{160,128},{224,1... | collective-permute-start | bytes 1179656 | tf_op jit(solution)/shard_map/ppermute | solution.py:382
  7.7 21.5 %collective-permute-start.4 = (bf16[2,96,1024]{2,1,0:T(8,128)(2,1)S(1)}, bf16[2,96,1024]{2,1,0:T(8,128)(2,1)S(1)}, u32[]{:S(2)}, u32[]{:S(2)}) collective-permute-start(bf16[2,96,1024]{2,1,0:T(8,128)(2,1)S(1)} %reshape.11.gr_ref), channel_id=1, source_target_pairs={{32,64},{96,128},{160,192},{64,32},{128,96},{192,160},{33,65},{97,... | collective-permute-start | bytes 1179656 | tf_op jit(solution)/shard_map/ppermute | solution.py:382
  17.8 14.5 %collective-permute-start.3 = (bf16[6,32,1024]{2,1,0:T(8,128)(2,1)S(1)}, bf16[6,32,1024]{2,1,0:T(8,128)(2,1)S(1)}, u32[]{:S(2)}, u32[]{:S(2)}) collective-permute-start(bf16[6,32,1024]{2,1,0:T(8,128)(2,1)S(1)} %shard_map.78.after_ref), channel_id=1, source_target_pairs={{1,2},{3,4},{5,6},{7,8},{9,10},{11,12},{13,14},{15,16},{17,18},{19... | collective-permute-start | bytes 1179656 | tf_op jit(solution)/shard_map/ppermute | solution.py:382
  28.2 1.6 %copy-start = (bf16[1024,1024]{1,0:T(8,128)(2,1)S(1)}, bf16[1024,1024]{1,0:T(8,128)(2,1)}, u32[]{:S(2)}) copy-start(bf16[1024,1024]{1,0:T(8,128)(2,1)} %get-tuple-element.36.wo_ref) | copy-start | bytes 6291460
  28.8 3.4 %collective-permute-start.2 = (bf16[6,32,1024]{2,1,0:T(8,128)(2,1)S(1)}, bf16[6,32,1024]{2,1,0:T(8,128)(2,1)S(1)}, u32[]{:S(2)}, u32[]{:S(2)}) collective-permute-start(bf16[6,32,1024]{2,1,0:T(8,128)(2,1)S(1)} %shard_map.80.after_ref), channel_id=1, source_target_pairs={{0,1},{2,3},{4,5},{6,7},{8,9},{10,11},{12,13},{14,15},{16,17},{18,... | collective-permute-start | bytes 1179656 | tf_op jit(solution)/shard_map/ppermute | solution.py:382
  42.0 9.3 %collective-permute-start.7 = (f32[12,4,256]{2,1,0:T(4,128)S(1)}, f32[12,4,256]{2,1,0:T(4,128)S(1)}, u32[]{:S(2)}, u32[]{:S(2)}) collective-permute-start(f32[12,4,256]{2,1,0:T(4,128)S(1)} %get-tuple-element.40), channel_id=1, source_target_pairs={{0,32},{64,96},{128,160},{192,224},{32,0},{96,64},{160,128},{224,1... | collective-permute-start | bytes 147464 | tf_op jit(solution)/shard_map/ppermute | solution.py:382
  44.5 6.9 %collective-permute-start.6 = (f32[12,4,256]{2,1,0:T(4,128)S(1)}, f32[12,4,256]{2,1,0:T(4,128)S(1)}, u32[]{:S(2)}, u32[]{:S(2)}) collective-permute-start(f32[12,4,256]{2,1,0:T(4,128)S(1)} %get-tuple-element.40), channel_id=1, source_target_pairs={{32,64},{96,128},{160,192},{64,32},{128,96},{192,160},{33,65},{97,... | collective-permute-start | bytes 147464 | tf_op jit(solution)/shard_map/ppermute | solution.py:382
  55.6 14.8 %collective-permute-start.8 = (bf16[2,32,1024]{2,1,0:T(8,128)(2,1)S(1)}, bf16[2,32,1024]{2,1,0:T(8,128)(2,1)S(1)}, u32[]{:S(2)}, u32[]{:S(2)}) collective-permute-start(bf16[2,32,1024]{2,1,0:T(8,128)(2,1)S(1)} %get-tuple-element.48), channel_id=1, source_target_pairs={{0,1},{2,3},{4,5},{6,7},{8,9},{10,11},{12,13},{14,15},{16,17},{18,... | collective-permute-start | bytes 393224 | tf_op jit(solution)/shard_map/ppermute | solution.py:382
  55.7 14.7 %collective-permute-start.9 = (bf16[2,32,1024]{2,1,0:T(8,128)(2,1)S(1)}, bf16[2,32,1024]{2,1,0:T(8,128)(2,1)S(1)}, u32[]{:S(2)}, u32[]{:S(2)}) collective-permute-start(bf16[2,32,1024]{2,1,0:T(8,128)(2,1)S(1)} %get-tuple-element.49), channel_id=1, source_target_pairs={{1,2},{3,4},{5,6},{7,8},{9,10},{11,12},{13,14},{15,16},{17,18},{19... | collective-permute-start | bytes 393224 | tf_op jit(solution)/shard_map/ppermute | solution.py:382

commit v2 on v1

--- a/solution.py
+++ b/solution.py
@@ -183,8 +183,6 @@
         for g in range(groups):
             krow_ref[side, g] = kh_ref[side, g, own]
             vrow_ref[side, g] = vh_ref[side, g, own]
-    dk_ref[...] = jnp.zeros_like(dk_ref)
-    dv_ref[...] = jnp.zeros_like(dv_ref)
     diag = (
         lax.broadcasted_iota(jnp.int32, (GW, GW), 0) // HD == lax.broadcasted_iota(jnp.int32, (GW, GW), 1) // 64
     )
@@ -250,8 +248,16 @@
             def middle(p):
                 return jnp.concatenate([p[(j * 6 + 2) * HALF : (j * 6 + 4) * HALF] for j in range(3)], axis=0)
 
-            dk_ref[g, rb : rb + 3] += nn(middle(ds), qs).reshape(3, 2 * HALF, GW)
-            dv_ref[g, rb : rb + 3] += nn(middle(pb), gs).reshape(3, 2 * HALF, GW)
+            def add(ref, y):
+                y = y.reshape(3, 2 * HALF, GW)
+                if rb == 0:
+                    ref[g, 0:3] = y
+                else:
+                    ref[g, rb : rb + 2] += y[:2]
+                    ref[g, rb + 2] = y[2]
+
+            add(dk_ref, nn(middle(ds), qs))
+            add(dv_ref, nn(middle(pb), gs))
 
         pipeline(3 * PER, scores, soft, back)
         return carry
@@ -324,8 +330,6 @@
     dka_ref, dva_ref,
 ):
     groups = k_ref.shape[0]
-    dka_ref[...] = dk_ref[:, 1:4]
-    dva_ref[...] = dv_ref[:, 1:4]
     reach = ((0, 2, 2 * HALF), (0, 3, 0), (1, 3, 0))
 
     def group(g, carry):
@@ -346,8 +350,19 @@
         def back(u, held):
             lo, hi, _ = reach[u // 2]
             qs, gs, pb, ds = held
-            dka_ref[g, lo:hi] += nn(ds, qs).reshape(hi - lo, 2 * HALF, GW)
-            dva_ref[g, lo:hi] += nn(pb, gs).reshape(hi - lo, 2 * HALF, GW)
+
+            def add(ref, first_ref, y):
+                y = y.reshape(hi - lo, 2 * HALF, GW)
+                if u == 0:
+                    ref[g, 0:2] = first_ref[g, 1:3] + y
+                elif u == 2:
+                    ref[g, 0:2] += y[:2]
+                    ref[g, 2] = first_ref[g, 3] + y[2]
+                else:
+                    ref[g, lo:hi] += y
+
+            add(dka_ref, dk_ref, nn(ds, qs))
+            add(dva_ref, dv_ref, nn(pb, gs))
 
         pipeline(6, scores, soft, back)
         return carry

time: 72.2 us -> 72.1 us (level)
  no operation moved by 1% of the time
where the time goes in v2:
time: 72.1 us; the launch traced here: 71.8 us
  starting transfers between devices  33.7 us (47%)
  Pallas kernels  32.9 us (46%)
  local copies, waits for them, and re-layouts  2.86 us (4%)
  waiting for transfers between devices  1.56 us (2%)
  between operations  0.82 us (1%)
    ppermute x10, starting transfers between devices, swap(): return lax.ppermute(block, axis, swap_pairs(lax.axis_size(axis), first))  33.7 us
    pallas_call x10, Pallas kernels, call(): pl.pallas_call(body, out_shape=[jax.ShapeDtypeStruct(s, d) for s, d in ou...  32.9 us
    ppermute x10, waiting for transfers between devices, swap(): return lax.ppermute(block, axis, swap_pairs(lax.axis_size(axis), first))  1.56 us
  transfers between devices with their start and end apart: 10, of which 2 were waited for; matrix products, arithmetic and copies ran while one was open for 2% of the time, Pallas kernels for 24%

profile of v2, /device:TPU:95, one launch (start us, length us, event | category | flops | bytes accessed | tf_op | source)
XLA Modules:
  0.0 71.8 jit_solution(10854553921748949654)
XLA Ops:
  0.6 1.1 %reshape.10.x_ref = bf16[2,96,1024]{2,1,0:T(8,128)(2,1)S(1)} reshape(bf16[2,24,4,1024]{3,2,1,0:T(4,128)(2,1)} %param.6) | data formatting | bytes 786432 | tf_op jit(solution)/shard_map/reshape | solution.py:409
  1.7 0.6 collective-permute-start.1
  2.4 4.1 %collective-permute-start = (bf16[2,96,1024]{2,1,0:T(8,128)(2,1)S(1)}, bf16[2,96,1024]{2,1,0:T(8,128)(2,1)S(1)}, u32[]{:S(2)}, u32[]{:S(2)}) collective-permute-start(bf16[2,96,1024]{2,1,0:T(8,128)(2,1)S(1)} %reshape.10.x_ref), channel_id=1, source_target_pairs={{32,64},{96,128},{160,192},{64,32},{128,96},{192,160},{33,65},{97,... | collective-permute-start | bytes 1179656 | tf_op jit(solution)/shard_map/ppermute | solution.py:397
  6.5 1.1 %reshape.11.gr_ref = bf16[2,96,1024]{2,1,0:T(8,128)(2,1)S(1)} reshape(bf16[2,24,4,1024]{3,2,1,0:T(4,128)(2,1)} %param.11) | data formatting | bytes 786432 | tf_op jit(solution)/shard_map/reshape | solution.py:412
  7.6 0.1 collective-permute-start.5
  7.7 4.0 %collective-permute-start.4 = (bf16[2,96,1024]{2,1,0:T(8,128)(2,1)S(1)}, bf16[2,96,1024]{2,1,0:T(8,128)(2,1)S(1)}, u32[]{:S(2)}, u32[]{:S(2)}) collective-permute-start(bf16[2,96,1024]{2,1,0:T(8,128)(2,1)S(1)} %reshape.11.gr_ref), channel_id=1, source_target_pairs={{32,64},{96,128},{160,192},{64,32},{128,96},{192,160},{33,65},{97,... | collective-permute-start | bytes 1179656 | tf_op jit(solution)/shard_map/ppermute | solution.py:397
  11.7 0.1 pad_add_fusion.info_ref
  11.8 5.4 %shard_map.77 = (bf16[4,3,64,256]{3,2,1,0:T(8,128)(2,1)S(1)}, bf16[4,3,64,256]{3,2,1,0:T(8,128)(2,1)S(1)}, bf16[4,3,64,256]{3,2,1,0:T(8,128)(2,1)S(1)}, bf16[4,3...) custom-call(s32[2]{0:T(128)S(1)} %pad_add_fusion.info_ref, ...), custom_call_target="tpu_custom_call" | custom-call | tf_op jit(solution)/shard_map/pallas_call | solution.py:38
  17.1 0.0 collective-permute-done.1.xb_ref
  17.2 0.0 collective-permute-done.xa_ref
  17.2 0.6 shard_map.78.after_ref
  17.8 7.8 %collective-permute-start.3 = (bf16[6,32,1024]{2,1,0:T(8,128)(2,1)S(1)}, bf16[6,32,1024]{2,1,0:T(8,128)(2,1)S(1)}, u32[]{:S(2)}, u32[]{:S(2)}) collective-permute-start(bf16[6,32,1024]{2,1,0:T(8,128)(2,1)S(1)} %shard_map.78.after_ref), channel_id=1, source_target_pairs={{1,2},{3,4},{5,6},{7,8},{9,10},{11,12},{13,14},{15,16},{17,18},{19... | collective-permute-start | bytes 1179656 | tf_op jit(solution)/shard_map/ppermute | solution.py:397
  25.6 2.6 %shard_map.79 = (bf16[4,2,3,64,256]{4,3,2,1,0:T(8,128)(2,1)S(1)}, bf16[4,2,3,64,256]{4,3,2,1,0:T(8,128)(2,1)S(1)}, bf16[4,2,3,64,256]{4,3,2,1,0:T(8,128)(2,1)S(1)}) custom-call(bf16[2,96,1024]{2,1,0:T(8,128)(2,1)S(1)} %collective-permute-done.xa_ref, bf16[2,96,1024]{2,1,0:T(8,128)(2,1)S(1)} %collective-permute-done.1.xb_ref, ...), custom_call_target="tpu_custom_call" | custom-call | tf_op jit(solution)/shard_map/pallas_call | solution.py:38
  28.2 0.6 shard_map.80.after_ref
  28.8 0.3 collective-permute-start.2
  29.1 0.0 collective-permute-done.5.gb_ref
  29.1 0.7 copy-done
  29.8 1.0 %shard_map.81.after_ref.gs_ref = bf16[4,2,3,64,256]{4,3,2,1,0:T(8,128)(2,1)S(1)} custom-call(bf16[2,96,1024]{2,1,0:T(8,128)(2,1)S(1)} %collective-permute-done.4.ga_ref, bf16[2,96,1024]{2,1,0:T(8,128)(2,1)S(1)} %collective-permute-done.5.gb_ref, bf16[1024,1024]{1,0:T(8,128)(2,1)S(1)} %copy-done, bf16[6,32,1024]{2,1,0:T(8,128)(2,1)S(1)} %shard_map.80.after_ref), custom_call_target="tpu_custom_call" | custom-call | tf_op jit(solution)/shard_map/pallas_call | solution.py:38
  30.8 1.4 %collective-permute-done.3.xo_ref = bf16[6,32,1024]{2,1,0:T(8,128)(2,1)S(1)} collective-permute-done((bf16[6,32,1024]{2,1,0:T(8,128)(2,1)S(1)}, bf16[6,32,1024]{2,1,0:T(8,128)(2,1)S(1)}, u32[]{:S(2)}, u32[]{:S(2)}) %collective-permute-start.3) | collective-permute-done | bytes 393248 | tf_op jit(solution)/shard_map/ppermute | solution.py:397
  32.2 0.0 collective-permute-done.2.xe_ref
  32.2 9.8 %shard_map.82 = (f32[12,4,256]{2,1,0:T(4,128)S(1)}, bf16[4,3,64,256]{3,2,1,0:T(8,128)(2,1)S(1)}, bf16[4,3,64,256]{3,2,1,0:T(8,128)(2,1)S(1)}, f32[4,5,64,256]{3,...) custom-call(s32[2]{0:T(128)S(1)} %pad_add_fusion.info_ref, ...), custom_call_target="tpu_custom_call" | custom-call | tf_op jit(solution)/shard_map/pallas_call | solution.py:38
  42.0 2.5 %collective-permute-start.7 = (f32[12,4,256]{2,1,0:T(4,128)S(1)}, f32[12,4,256]{2,1,0:T(4,128)S(1)}, u32[]{:S(2)}, u32[]{:S(2)}) collective-permute-start(f32[12,4,256]{2,1,0:T(4,128)S(1)} %get-tuple-element.40), channel_id=1, source_target_pairs={{0,32},{64,96},{128,160},{192,224},{32,0},{96,64},{160,128},{224,1... | collective-permute-start | bytes 147464 | tf_op jit(solution)/shard_map/ppermute | solution.py:397
  44.5 5.4 %collective-permute-start.6 = (f32[12,4,256]{2,1,0:T(4,128)S(1)}, f32[12,4,256]{2,1,0:T(4,128)S(1)}, u32[]{:S(2)}, u32[]{:S(2)}) collective-permute-start(f32[12,4,256]{2,1,0:T(4,128)S(1)} %get-tuple-element.40), channel_id=1, source_target_pairs={{32,64},{96,128},{160,192},{64,32},{128,96},{192,160},{33,65},{97,... | collective-permute-start | bytes 147464 | tf_op jit(solution)/shard_map/ppermute | solution.py:397
  49.9 1.4 %shard_map.83 = (bf16[2,24,4,1024]{3,2,1,0:T(4,128)(2,1)}, f32[3,64,1024]{2,1,0:T(8,128)S(1)}) custom-call(bf16[4,3,64,256]{3,2,1,0:T(8,128)(2,1)S(1)} %get-tuple-element.37.mixed_ref, bf16[4,3,64,256]{3,2,1,0:T(8,128)(2,1)S(1)} %get-tuple-element.38.dq_ref, bf16[1024,1024]{1,0:T(8,128)(2,1)S(1)} %copy-done, bf16[1024,1024]{1,0:T(8,128)(2,1)S(1)} %get-tuple-element.26.wq_ref), custom_call_target="tpu_custom_call" | custom-call | tf_op jit(solution)/shard_map/pallas_call | solution.py:38
  51.3 0.0 collective-permute-done.7.sb_ref
  51.3 0.1 collective-permute-done.6.sa_ref
  51.4 4.2 %shard_map.85 = (bf16[2,32,1024]{2,1,0:T(8,128)(2,1)S(1)}, bf16[2,32,1024]{2,1,0:T(8,128)(2,1)S(1)}) custom-call(s32[2]{0:T(128)S(1)} %pad_add_fusion.info_ref, f32[12,4,256]{2,1,0:T(4,128)S(1)} %collective-permute-done.6.sa_ref, f32[12,4,256]{2,1,0:T(4,128)S(1)} %collective-permute-done.7.sb_ref, bf16[4,2,3,64,256]{4,3,2,1,0:T(8,128)(2,1)S(1)} %get-tuple-element.41.qs_ref, ...), custom_call_target="tpu_custom_call" | custom-call | tf_op jit(solution)/shard_map/pallas_call | solution.py:38
  55.6 0.1 collective-permute-start.8
  55.7 8.7 %collective-permute-start.9 = (bf16[2,32,1024]{2,1,0:T(8,128)(2,1)S(1)}, bf16[2,32,1024]{2,1,0:T(8,128)(2,1)S(1)}, u32[]{:S(2)}, u32[]{:S(2)}) collective-permute-start(bf16[2,32,1024]{2,1,0:T(8,128)(2,1)S(1)} %get-tuple-element.49), channel_id=1, source_target_pairs={{1,2},{3,4},{5,6},{7,8},{9,10},{11,12},{13,14},{15,16},{17,18},{19... | collective-permute-start | bytes 393224 | tf_op jit(solution)/shard_map/ppermute | solution.py:397
  64.5 5.9 %shard_map.84.own_ref = f32[2,96,1024]{2,1,0:T(8,128)S(1)} custom-call(f32[12,4,256]{2,1,0:T(4,128)S(1)} %collective-permute-done.6.sa_ref, f32[12,4,256]{2,1,0:T(4,128)S(1)} %collective-permute-done.7.sb_ref, bf16[4,2,3,64,256]{4,3,2,1,0:T(8,128)(2,1)S(1)} %get-tuple-element.41.qs_ref, bf16[4,2,3,64,256]{4,3,2,1,0:T(8,128)(2,1)S(1)} %shard_map.81.after_ref.gs_ref, ...), custom_call_target="tpu_custom_call" | custom-call | tf_op jit(solution)/shard_map/pallas_call | solution.py:38
  70.4 0.0 collective-permute-done.8.re_ref
  70.4 1.4 %shard_map.86 = bf16[2,24,4,1024]{3,2,1,0:T(4,128)(2,1)} custom-call(s32[2]{0:T(128)S(1)} %pad_add_fusion.info_ref, f32[2,96,1024]{2,1,0:T(8,128)S(1)} %shard_map.84.own_ref, bf16[2,32,1024]{2,1,0:T(8,128)(2,1)S(1)} %collective-permute-done.8.re_ref, bf16[2,32,1024]{2,1,0:T(8,128)(2,1)S(1)} %collective-permute-done.9.ro_ref), custom_call_target="tpu_custom_call" | custom-call | tf_op jit(solution)/shard_map/pallas_call | solution.py:38
  (3 shorter events, 0.0 us)
Async XLA Ops:
  1.7 15.4 %collective-permute-start.1 = (bf16[2,96,1024]{2,1,0:T(8,128)(2,1)S(1)}, bf16[2,96,1024]{2,1,0:T(8,128)(2,1)S(1)}, u32[]{:S(2)}, u32[]{:S(2)}) collective-permute-start(bf16[2,96,1024]{2,1,0:T(8,128)(2,1)S(1)} %reshape.10.x_ref), channel_id=1, source_target_pairs={{0,32},{64,96},{128,160},{192,224},{32,0},{96,64},{160,128},{224,1... | collective-permute-start | bytes 1179656 | tf_op jit(solution)/shard_map/ppermute | solution.py:397
  2.4 14.8 %collective-permute-start = (bf16[2,96,1024]{2,1,0:T(8,128)(2,1)S(1)}, bf16[2,96,1024]{2,1,0:T(8,128)(2,1)S(1)}, u32[]{:S(2)}, u32[]{:S(2)}) collective-permute-start(bf16[2,96,1024]{2,1,0:T(8,128)(2,1)S(1)} %reshape.10.x_ref), channel_id=1, source_target_pairs={{32,64},{96,128},{160,192},{64,32},{128,96},{192,160},{33,65},{97,... | collective-permute-start | bytes 1179656 | tf_op jit(solution)/shard_map/ppermute | solution.py:397
  7.6 21.6 %collective-permute-start.5 = (bf16[2,96,1024]{2,1,0:T(8,128)(2,1)S(1)}, bf16[2,96,1024]{2,1,0:T(8,128)(2,1)S(1)}, u32[]{:S(2)}, u32[]{:S(2)}) collective-permute-start(bf16[2,96,1024]{2,1,0:T(8,128)(2,1)S(1)} %reshape.11.gr_ref), channel_id=1, source_target_pairs={{0,32},{64,96},{128,160},{192,224},{32,0},{96,64},{160,128},{224,1... | collective-permute-start | bytes 1179656 | tf_op jit(solution)/shard_map/ppermute | solution.py:397
  7.7 21.5 %collective-permute-start.4 = (bf16[2,96,1024]{2,1,0:T(8,128)(2,1)S(1)}, bf16[2,96,1024]{2,1,0:T(8,128)(2,1)S(1)}, u32[]{:S(2)}, u32[]{:S(2)}) collective-permute-start(bf16[2,96,1024]{2,1,0:T(8,128)(2,1)S(1)} %reshape.11.gr_ref), channel_id=1, source_target_pairs={{32,64},{96,128},{160,192},{64,32},{128,96},{192,160},{33,65},{97,... | collective-permute-start | bytes 1179656 | tf_op jit(solution)/shard_map/ppermute | solution.py:397
  17.8 14.5 %collective-permute-start.3 = (bf16[6,32,1024]{2,1,0:T(8,128)(2,1)S(1)}, bf16[6,32,1024]{2,1,0:T(8,128)(2,1)S(1)}, u32[]{:S(2)}, u32[]{:S(2)}) collective-permute-start(bf16[6,32,1024]{2,1,0:T(8,128)(2,1)S(1)} %shard_map.78.after_ref), channel_id=1, source_target_pairs={{1,2},{3,4},{5,6},{7,8},{9,10},{11,12},{13,14},{15,16},{17,18},{19... | collective-permute-start | bytes 1179656 | tf_op jit(solution)/shard_map/ppermute | solution.py:397
  28.2 1.6 %copy-start = (bf16[1024,1024]{1,0:T(8,128)(2,1)S(1)}, bf16[1024,1024]{1,0:T(8,128)(2,1)}, u32[]{:S(2)}) copy-start(bf16[1024,1024]{1,0:T(8,128)(2,1)} %get-tuple-element.36.wo_ref) | copy-start | bytes 6291460
  28.8 3.4 %collective-permute-start.2 = (bf16[6,32,1024]{2,1,0:T(8,128)(2,1)S(1)}, bf16[6,32,1024]{2,1,0:T(8,128)(2,1)S(1)}, u32[]{:S(2)}, u32[]{:S(2)}) collective-permute-start(bf16[6,32,1024]{2,1,0:T(8,128)(2,1)S(1)} %shard_map.80.after_ref), channel_id=1, source_target_pairs={{0,1},{2,3},{4,5},{6,7},{8,9},{10,11},{12,13},{14,15},{16,17},{18,... | collective-permute-start | bytes 1179656 | tf_op jit(solution)/shard_map/ppermute | solution.py:397
  42.0 9.3 %collective-permute-start.7 = (f32[12,4,256]{2,1,0:T(4,128)S(1)}, f32[12,4,256]{2,1,0:T(4,128)S(1)}, u32[]{:S(2)}, u32[]{:S(2)}) collective-permute-start(f32[12,4,256]{2,1,0:T(4,128)S(1)} %get-tuple-element.40), channel_id=1, source_target_pairs={{0,32},{64,96},{128,160},{192,224},{32,0},{96,64},{160,128},{224,1... | collective-permute-start | bytes 147464 | tf_op jit(solution)/shard_map/ppermute | solution.py:397
  44.5 6.9 %collective-permute-start.6 = (f32[12,4,256]{2,1,0:T(4,128)S(1)}, f32[12,4,256]{2,1,0:T(4,128)S(1)}, u32[]{:S(2)}, u32[]{:S(2)}) collective-permute-start(f32[12,4,256]{2,1,0:T(4,128)S(1)} %get-tuple-element.40), channel_id=1, source_target_pairs={{32,64},{96,128},{160,192},{64,32},{128,96},{192,160},{33,65},{97,... | collective-permute-start | bytes 147464 | tf_op jit(solution)/shard_map/ppermute | solution.py:397
  55.6 14.7 %collective-permute-start.8 = (bf16[2,32,1024]{2,1,0:T(8,128)(2,1)S(1)}, bf16[2,32,1024]{2,1,0:T(8,128)(2,1)S(1)}, u32[]{:S(2)}, u32[]{:S(2)}) collective-permute-start(bf16[2,32,1024]{2,1,0:T(8,128)(2,1)S(1)} %get-tuple-element.48), channel_id=1, source_target_pairs={{0,1},{2,3},{4,5},{6,7},{8,9},{10,11},{12,13},{14,15},{16,17},{18,... | collective-permute-start | bytes 393224 | tf_op jit(solution)/shard_map/ppermute | solution.py:397
  55.7 14.6 %collective-permute-start.9 = (bf16[2,32,1024]{2,1,0:T(8,128)(2,1)S(1)}, bf16[2,32,1024]{2,1,0:T(8,128)(2,1)S(1)}, u32[]{:S(2)}, u32[]{:S(2)}) collective-permute-start(bf16[2,32,1024]{2,1,0:T(8,128)(2,1)S(1)} %get-tuple-element.49), channel_id=1, source_target_pairs={{1,2},{3,4},{5,6},{7,8},{9,10},{11,12},{13,14},{15,16},{17,18},{19... | collective-permute-start | bytes 393224 | tf_op jit(solution)/shard_map/ppermute | solution.py:397
